TPU v7x, 32 devices: a whole 2x2x4 slice. The times are simulated.
32 devices in a mesh: xy: 16 (over z, x, core), gz: 2 (over y).
Axes of the slice: x: 2, y: 2, z: 4, core: 2. Of those that a mesh axis runs over, the one named last changes fastest.
Arguments:
- previous: float32 [256, 128, 256], P('xy', 'gz'), may hold values from -2.1 to 2.1
- current: float32 [256, 128, 256], P('xy', 'gz'), may hold values from -1.8 to 1.8
- stiffness: float32 [256, 128, 256], P('xy', 'gz'), may hold values from 0.05 to 0.2
- buoyancy: float32 [256, 128, 256], P('xy', 'gz'), may hold values from 0.5 to 1
Outputs:
- next_field: float32 [256, 128, 256], P('xy', 'gz')
- coefficients: float32 [128, 64, 128], P(('xy', 'gz'))
All inputs are finite; a program needn't handle non-finite values.
Results may differ from a plain program's by a relative error of at most 0.00002.
Values sent between devices are 32-bit elements; how exact they have to be, the bound alone decides.
A program may use at most 64 MiB of HBM per device.

v0:
```python
import jax
import jax.numpy as jnp
from jax import lax
from jax.sharding import PartitionSpec as P

coeffs = (1225.0 / 1024.0, -245.0 / 3072.0, 49.0 / 5120.0, -5.0 / 7168.0)
alpha_lift = -1.586134342
beta_lift = -0.05298011854
gamma_lift = 0.8829110762
delta_lift = 0.4435068522
wavelet_scale = 1.149604398


def padded_2(cells, sides, width):
    for axis, dim in sides:
        count = lax.axis_size(axis)
        ends = count - 1
        head = lax.slice_in_dim(cells, 0, width, axis=dim)
        tail = lax.slice_in_dim(cells, cells.shape[dim] - width, cells.shape[dim], axis=dim)
        cells = jnp.concatenate(
            [
                lax.ppermute(tail, axis, [(i, (i + 1) % count) for i in range(ends)]),
                cells,
                lax.ppermute(head, axis, [((i + 1) % count, i) for i in range(ends)]),
            ],
            axis=dim,
        )
    return cells


def cut_along(source, begin_at, length, sweep_direction):
    return lax.slice_in_dim(source, begin_at, begin_at + length, axis=sweep_direction)


def compute_flux(
    padded, bpadded, sweep_direction, margin, first_face, end_face, first_global, extent
):
    length = end_face - first_face
    gradient = None
    for term_index, weight in enumerate(coeffs):
        offset = term_index + 1
        summand = weight * (
            cut_along(padded, first_face + offset + margin, length, sweep_direction)
            - cut_along(padded, first_face + 1 - offset + margin, length, sweep_direction)
        )
        gradient = summand if gradient is None else gradient + summand
    face_buoy = 0.5 * (
        cut_along(bpadded, first_face + margin, length, sweep_direction)
        + cut_along(bpadded, first_face + 1 + margin, length, sweep_direction)
    )
    face_ids = (
        lax.broadcasted_iota(jnp.int32, gradient.shape, sweep_direction) + first_face + first_global
    )
    inside = (face_ids >= 0) & (face_ids <= extent - 2)
    return jnp.where(inside, face_buoy * gradient, jnp.float32(0.0))


def diverge(flux_faces, sweep_direction, length):
    result = None
    for term_index, weight in enumerate(coeffs):
        offset = term_index + 1
        summand = weight * (
            cut_along(flux_faces, offset + 3, length, sweep_direction)
            - cut_along(flux_faces, 4 - offset, length, sweep_direction)
        )
        result = summand if result is None else result + summand
    return result


def shift_next(sample_values, sweep_direction):
    length = sample_values.shape[sweep_direction]
    return jnp.concatenate(
        [
            cut_along(sample_values, 1, length - 1, sweep_direction),
            cut_along(sample_values, length - 1, 1, sweep_direction),
        ],
        axis=sweep_direction,
    )


def shift_prev(sample_values, sweep_direction):
    length = sample_values.shape[sweep_direction]
    return jnp.concatenate(
        [
            cut_along(sample_values, 0, 1, sweep_direction),
            cut_along(sample_values, 0, length - 1, sweep_direction),
        ],
        axis=sweep_direction,
    )


def lift_line(sample_values, sweep_direction):
    length = sample_values.shape[sweep_direction]
    even_samples = lax.slice_in_dim(sample_values, 0, length, 2, axis=sweep_direction)
    odd_samples = lax.slice_in_dim(sample_values, 1, length, 2, axis=sweep_direction)
    odd_samples = odd_samples + alpha_lift * (
        even_samples + shift_next(even_samples, sweep_direction)
    )
    even_samples = even_samples + beta_lift * (
        shift_prev(odd_samples, sweep_direction) + odd_samples
    )
    odd_samples = odd_samples + gamma_lift * (
        even_samples + shift_next(even_samples, sweep_direction)
    )
    even_samples = even_samples + delta_lift * (
        shift_prev(odd_samples, sweep_direction) + odd_samples
    )
    return jnp.stack(
        (even_samples * wavelet_scale, odd_samples / wavelet_scale), axis=sweep_direction + 1
    ).reshape(sample_values.shape)


def depth_levels(sample_values):
    for depth_level in range(4):
        stride = 2**depth_level
        portion = sample_values[:, ::stride, :]
        sample_values = sample_values.at[:, ::stride, :].set(lift_line(portion, 1))
    return sample_values


def mirror_lift(sample_values):
    length = sample_values.shape[0]
    rim_ext = padded_2(sample_values, (("xy", 0),), 4)
    position = lax.axis_index("xy")
    devices = lax.axis_size("xy")
    low_mirror = jnp.flip(rim_ext[5:9], 0)
    high_mirror = jnp.flip(rim_ext[length - 1 : length + 3], 0)
    lower = jnp.where(position == 0, low_mirror, rim_ext[:4])
    upper = jnp.where(position == devices - 1, high_mirror, rim_ext[length + 4 :])
    extended = jnp.concatenate([lower, rim_ext[4 : length + 4], upper], axis=0)
    even_samples = extended[0::2]
    odd_samples = extended[1::2]
    odd_one = odd_samples[:-1] + alpha_lift * (even_samples[:-1] + even_samples[1:])
    even_two = even_samples[1:-1] + beta_lift * (odd_one[:-1] + odd_one[1:])
    odd_triple = odd_one[1:-1] + gamma_lift * (even_two[:-1] + even_two[1:])
    even_quartet = even_two[1:-1] + delta_lift * (odd_triple[:-1] + odd_triple[1:])
    return jnp.stack(
        (even_quartet * wavelet_scale, odd_triple[1:] / wavelet_scale), axis=1
    ).reshape(sample_values.shape)


def on_device(previous, current, stiffness, buoyancy):
    rows_x, rows_z, rows_y = current.shape
    start_x = lax.axis_index("xy") * rows_x
    start_z = lax.axis_index("gz") * rows_z
    extent_x = lax.axis_size("xy") * rows_x
    extent_z = lax.axis_size("gz") * rows_z
    side_pad = ((0, 0), (0, 0), (7, 7))
    flux_y = compute_flux(
        jnp.pad(current, side_pad), jnp.pad(buoyancy, side_pad), 2, 7, -4, rows_y + 3, 0, rows_y
    )
    across_y = diverge(flux_y, 2, rows_y)
    padded, bpadded = (
        padded_2(current, (("xy", 0), ("gz", 1)), 4),
        padded_2(buoyancy, (("xy", 0), ("gz", 1)), 4),
    )
    local_x = compute_flux(
        padded[:, 4 : 4 + rows_z], bpadded[:, 4 : 4 + rows_z], 0, 4, 0, rows_x, start_x, extent_x
    )
    local_z = compute_flux(
        padded[4 : 4 + rows_x], bpadded[4 : 4 + rows_x], 1, 4, 0, rows_z, start_z, extent_z
    )
    flux_x = padded_2(local_x, (("xy", 0),), 4)
    flux_z = padded_2(local_z, (("gz", 1),), 4)
    laplace_sum = diverge(flux_x, 0, rows_x) + diverge(flux_z, 1, rows_z) + across_y
    next_field = 2.0 * current - previous + stiffness * laplace_sum
    snapshot = next_field[::2, ::2, ::2]
    planar = lift_line(mirror_lift(snapshot), 2)
    corner = planar[::2, :, ::2]
    corner = lift_line(mirror_lift(corner), 2)
    planar = planar.at[::2, :, ::2].set(corner)
    coefficients = depth_levels(
        lax.all_to_all(planar, "gz", split_axis=0, concat_axis=1, tiled=True)
    )
    return (next_field, coefficients)


def solution(mesh):
    return jax.shard_map(
        on_device,
        mesh=mesh,
        in_specs=(
            P("xy", "gz", None),
            P("xy", "gz", None),
            P("xy", "gz", None),
            P("xy", "gz", None),
        ),
        out_specs=(P("xy", "gz", None), P(("xy", "gz"), None, None)),
        check_vma=False,
    )
```

profile of v0, /device:TPU:11, one launch (start us, length us, event | category | flops | bytes accessed | tf_op | source)
XLA Modules:
  0.0 121.7 jit_solution(12538053801963381577)
XLA Ops:
  0.7 2.0 %fusion.182 = (f32[4,64,256]{2,1,0:T(8,128)}, f32[4,64,256]{2,1,0:T(8,128)}) fusion(f32[16,64,256]{2,1,0:T(8,128)} %param.9), kind=kLoop, calls=%fused_computation.315 | loop fusion | bytes 1048576 | tf_op jit(solution)/shard_map/slice | solution.py:18
  2.6 3.7 %collective-permute-start.2 = (f32[4,64,256]{2,1,0:T(8,128)}, f32[4,64,256]{2,1,0:T(8,128)S(1)}, u32[]{:S(2)}, u32[]{:S(2)}) collective-permute-start(f32[4,64,256]{2,1,0:T(8,128)} %get-tuple-element.56), channel_id=1, source_target_pairs={{0,2},{2,4},{4,6},{6,8},{8,10},{10,12},{12,14},{14,16},{16,18},{18... | collective-permute-start | bytes 786440 | tf_op jit(solution)/shard_map/ppermute | solution.py:22
  6.4 1.9 %collective-permute-start.1 = (f32[4,64,256]{2,1,0:T(8,128)}, f32[4,64,256]{2,1,0:T(8,128)S(1)}, u32[]{:S(2)}, u32[]{:S(2)}) collective-permute-start(f32[4,64,256]{2,1,0:T(8,128)} %get-tuple-element.55), channel_id=1, source_target_pairs={{2,0},{4,2},{6,4},{8,6},{10,8},{12,10},{14,12},{16,14},{18,16},{20... | collective-permute-start | bytes 786440 | tf_op jit(solution)/shard_map/ppermute | solution.py:24
  8.3 1.9 %fusion.181 = (f32[4,64,256]{2,1,0:T(8,128)}, f32[4,64,256]{2,1,0:T(8,128)}) fusion(f32[16,64,256]{2,1,0:T(8,128)} %param.11), kind=kLoop, calls=%fused_computation.314 | loop fusion | bytes 1048576 | tf_op jit(solution)/shard_map/slice | solution.py:18
  10.2 2.5 %collective-permute-start = (f32[4,64,256]{2,1,0:T(8,128)}, f32[4,64,256]{2,1,0:T(8,128)S(1)}, u32[]{:S(2)}, u32[]{:S(2)}) collective-permute-start(f32[4,64,256]{2,1,0:T(8,128)} %get-tuple-element.53), channel_id=1, source_target_pairs={{2,0},{4,2},{6,4},{8,6},{10,8},{12,10},{14,12},{16,14},{18,16},{20... | collective-permute-start | bytes 786440 | tf_op jit(solution)/shard_map/ppermute | solution.py:24
  12.7 4.0 %collective-permute-start.5 = (f32[4,64,256]{2,1,0:T(8,128)}, f32[4,64,256]{2,1,0:T(8,128)}, u32[]{:S(2)}, u32[]{:S(2)}) collective-permute-start(f32[4,64,256]{2,1,0:T(8,128)} %get-tuple-element.54), channel_id=1, source_target_pairs={{0,2},{2,4},{4,6},{6,8},{8,10},{10,12},{12,14},{14,16},{16,18},{18... | collective-permute-start | bytes 786440 | tf_op jit(solution)/shard_map/ppermute | solution.py:22
  16.7 3.8 %fusion.3 = f32[16,64,263]{2,1,0:T(8,128)S(1)} fusion(f32[16,64,256]{2,1,0:T(8,128)S(1)} %copy-done.1, f32[16,64,256]{2,1,0:T(8,128)S(1)} %copy-done, pred[263]{0:T(512)(128)(4,1)S(1)} %fusion.171), kind=kLoop, calls=%fused_computation.37 | loop fusion | flops 4039680 | bytes 3174663 | tf_op jit(solution)/shard_map/jit(_where)/select_n | solution.py:55
  21.1 1.0 constant_dynamic-update-slice_fusion.6
  24.1 1.3 %collective-permute-start.7 = (f32[24,4,256]{2,1,0:T(4,128)S(1)}, f32[24,4,256]{2,1,0:T(4,128)S(1)}, u32[]{:S(2)}, u32[]{:S(2)}) collective-permute-start(f32[24,4,256]{2,1,0:T(4,128)S(1)} %get-tuple-element.42), channel_id=1, source_target_pairs={{1,0},{3,2},{5,4},{7,6},{9,8},{11,10},{13,12},{15,14},{17,16},{19,... | collective-permute-start | bytes 294920 | tf_op jit(solution)/shard_map/ppermute | solution.py:24
  25.4 4.0 %collective-permute-start.8 = (f32[24,4,256]{2,1,0:T(4,128)S(1)}, f32[24,4,256]{2,1,0:T(4,128)S(1)}, u32[]{:S(2)}, u32[]{:S(2)}) collective-permute-start(f32[24,4,256]{2,1,0:T(4,128)S(1)} %get-tuple-element.43), channel_id=1, source_target_pairs={{0,1},{2,3},{4,5},{6,7},{8,9},{10,11},{12,13},{14,15},{16,17},{18,... | collective-permute-start | bytes 294920 | tf_op jit(solution)/shard_map/ppermute | solution.py:22
  29.5 1.3 %collective-permute-start.6 = (f32[24,4,256]{2,1,0:T(4,128)S(1)}, f32[24,4,256]{2,1,0:T(4,128)S(1)}, u32[]{:S(2)}, u32[]{:S(2)}) collective-permute-start(f32[24,4,256]{2,1,0:T(4,128)S(1)} %slice.723), channel_id=1, source_target_pairs={{1,0},{3,2},{5,4},{7,6},{9,8},{11,10},{13,12},{15,14},{17,16},{19,... | collective-permute-start | bytes 294920 | tf_op jit(solution)/shard_map/ppermute | solution.py:24
  30.8 5.0 %collective-permute-start.3 = (f32[4,64,256]{2,1,0:T(8,128)S(1)}, f32[4,64,256]{2,1,0:T(8,128)S(1)}, u32[]{:S(2)}, u32[]{:S(2)}) collective-permute-start(f32[4,64,256]{2,1,0:T(8,128)S(1)} %get-tuple-element.44), channel_id=1, source_target_pairs={{0,2},{2,4},{4,6},{6,8},{8,10},{10,12},{12,14},{14,16},{16,18},{18... | collective-permute-start | bytes 786440 | tf_op jit(solution)/shard_map/ppermute | solution.py:22
  35.8 1.9 %collective-permute-start.4 = (f32[4,64,256]{2,1,0:T(8,128)S(1)}, f32[4,64,256]{2,1,0:T(8,128)}, u32[]{:S(2)}, u32[]{:S(2)}) collective-permute-start(f32[4,64,256]{2,1,0:T(8,128)S(1)} %get-tuple-element.45), channel_id=1, source_target_pairs={{2,0},{4,2},{6,4},{8,6},{10,8},{12,10},{14,12},{16,14},{18,16},{20... | collective-permute-start | bytes 786440 | tf_op jit(solution)/shard_map/ppermute | solution.py:24
  37.8 2.2 %fusion.53 = f32[16,64,256]{2,1,0:T(8,128)S(1)} fusion(f32[24,64,256]{2,1,0:T(8,128)S(1)} %constant_dynamic-update-slice_fusion.7, f32[16,64,256]{2,1,0:T(8,128)S(1)} %copy-done, f32[24,4,256]{2,1,0:T(4,128)S(1)} %collective-permute-done.8, f32[24,4,256]{2,1,0:T(4,128)S(1)} %collective-permute-done.7, f32[16,64,256]{2,1,0:T(8,128)S(1)} %copy-done.2, ...), kind=kLoop, calls=%fused_computation.97 | loop fusion | flops 6029312 | bytes 6586432 | tf_op jit(solution)/shard_map/jit(_where)/select_n | solution.py:55
  41.0 1.3 %collective-permute-start.10 = (f32[16,4,256]{2,1,0:T(4,128)}, f32[16,4,256]{2,1,0:T(4,128)S(1)}, u32[]{:S(2)}, u32[]{:S(2)}) collective-permute-start(f32[16,4,256]{2,1,0:T(4,128)} %get-tuple-element.47), channel_id=1, source_target_pairs={{1,0},{3,2},{5,4},{7,6},{9,8},{11,10},{13,12},{15,14},{17,16},{19,... | collective-permute-start | bytes 196616 | tf_op jit(solution)/shard_map/ppermute | solution.py:24
  42.3 4.3 %collective-permute-start.9 = (f32[16,4,256]{2,1,0:T(4,128)}, f32[16,4,256]{2,1,0:T(4,128)S(1)}, u32[]{:S(2)}, u32[]{:S(2)}) collective-permute-start(f32[16,4,256]{2,1,0:T(4,128)} %get-tuple-element.46), channel_id=1, source_target_pairs={{0,1},{2,3},{4,5},{6,7},{8,9},{10,11},{12,13},{14,15},{16,17},{18,... | collective-permute-start | bytes 196616 | tf_op jit(solution)/shard_map/ppermute | solution.py:22
  46.6 1.5 %collective-permute-done.9 = f32[16,4,256]{2,1,0:T(4,128)S(1)} collective-permute-done((f32[16,4,256]{2,1,0:T(4,128)}, f32[16,4,256]{2,1,0:T(4,128)S(1)}, u32[]{:S(2)}, u32[]{:S(2)}) %collective-permute-start.9) | collective-permute-done | bytes 65568 | tf_op jit(solution)/shard_map/ppermute | solution.py:22
  48.2 11.3 %fusion.23 = f32[16,64,256]{2,1,0:T(8,128)} fusion(f32[16,64,256]{2,1,0:T(8,128)} %param.10, f32[16,64,256]{2,1,0:T(8,128)} %copy-done.4, f32[16,64,256]{2,1,0:T(8,128)} %copy-done.3, f32[16,4,256]{2,1,0:T(4,128)S(1)} %collective-permute-done.10, f32[4,64,256]{2,1,0:T(8,128)} %collective-permute-done.4, f32[16,4,256]{2,1,0:T(4,128)S(1)} %collective-permute-done.9, ...), kind=kLoop, calls=%fused_computation.67 | loop fusion | flops 13893632 | bytes 15335424 | tf_op jit(solution)/shard_map/add | solution.py:166
  59.5 6.7 %slice.603 = f32[8,32,128]{2,1,0:T(8,128)S(1)} slice(f32[16,64,256]{2,1,0:T(8,128)} %fusion.23), slice={[0:16:2], [0:64:2], [0:256:2]} | slice | bytes 262144 | tf_op jit(solution)/shard_map/slice | solution.py:167
  66.2 5.4 %collective-permute-start.11 = (f32[4,32,128]{2,1,0:T(8,128)S(1)}, f32[4,32,128]{2,1,0:T(8,128)S(1)}, u32[]{:S(2)}, u32[]{:S(2)}) collective-permute-start(f32[4,32,128]{2,1,0:T(8,128)S(1)} %get-tuple-element.68), channel_id=1, source_target_pairs={{0,2},{2,4},{4,6},{6,8},{8,10},{10,12},{12,14},{14,16},{16,18},{18... | collective-permute-start | bytes 196616 | tf_op jit(solution)/shard_map/ppermute | solution.py:22
  71.6 1.9 %collective-permute-start.12 = (f32[4,32,128]{2,1,0:T(8,128)S(1)}, f32[4,32,128]{2,1,0:T(8,128)S(1)}, u32[]{:S(2)}, u32[]{:S(2)}) collective-permute-start(f32[4,32,128]{2,1,0:T(8,128)S(1)} %get-tuple-element.66), channel_id=1, source_target_pairs={{2,0},{4,2},{6,4},{8,6},{10,8},{12,10},{14,12},{16,14},{18,16},{20... | collective-permute-start | bytes 196616 | tf_op jit(solution)/shard_map/ppermute | solution.py:24
  73.6 4.5 %collective-permute-done.12 = f32[4,32,128]{2,1,0:T(8,128)S(1)} collective-permute-done((f32[4,32,128]{2,1,0:T(8,128)S(1)}, f32[4,32,128]{2,1,0:T(8,128)S(1)}, u32[]{:S(2)}, u32[]{:S(2)}) %collective-permute-start.12) | collective-permute-done | bytes 65568 | tf_op jit(solution)/shard_map/ppermute | solution.py:24
  78.3 2.3 %slice.622 = f32[8,32,64]{2,1,0:T(8,128)S(1)} slice(f32[8,32,128]{2,1,0:T(8,128)S(1)} %bitcast.84), slice={[0:8:1], [0:32:1], [0:128:2]} | slice | bytes 131072 | tf_op jit(solution)/shard_map/slice | solution.py:94
  80.9 2.4 %slice.623 = f32[8,32,64]{2,1,0:T(8,128)S(1)} slice(f32[8,32,128]{2,1,0:T(8,128)S(1)} %bitcast.85), slice={[0:8:1], [0:32:1], [1:128:2]} | slice | bytes 131072 | tf_op jit(solution)/shard_map/slice | solution.py:95
  84.3 1.9 %collective-permute-start.13 = (f32[4,32,64]{1,2,0:T(8,128)S(1)}, f32[4,32,64]{1,2,0:T(8,128)S(1)}, u32[]{:S(2)}, u32[]{:S(2)}) collective-permute-start(f32[4,32,64]{1,2,0:T(8,128)S(1)} %slice.632), channel_id=1, source_target_pairs={{2,0},{4,2},{6,4},{8,6},{10,8},{12,10},{14,12},{16,14},{18,16},{20... | collective-permute-start | bytes 98312 | tf_op jit(solution)/shard_map/ppermute | solution.py:24
  86.4 4.7 %collective-permute-start.14 = (f32[4,32,64]{1,2,0:T(8,128)S(1)}, f32[4,32,64]{1,2,0:T(8,128)S(1)}, u32[]{:S(2)}, u32[]{:S(2)}) collective-permute-start(f32[4,32,64]{1,2,0:T(8,128)S(1)} %slice.632), channel_id=1, source_target_pairs={{0,2},{2,4},{4,6},{6,8},{8,10},{10,12},{12,14},{14,16},{16,18},{18... | collective-permute-start | bytes 98312 | tf_op jit(solution)/shard_map/ppermute | solution.py:22
  91.6 1.2 collective-permute-done.14
  95.3 12.5 %scatter_fusion = f32[8,32,128]{1,2,0:T(8,128)S(1)} fusion(f32[8,32,128]{1,2,0:T(8,128)S(1)} %bitcast.75, s32[256]{0:T(256)S(1)} %reshape.87, f32[256,32]{1,0:T(8,128)S(1)} %bitcast.95), kind=kCustom, calls=%fused_computation | custom fusion | bytes 100352 | tf_op jit(solution)/shard_map/scatter | solution.py:171
  108.6 3.4 %all-to-all-start = ((f32[8,32,128]{2,1,0:T(8,128)}), f32[8,32,128]{2,1,0:T(8,128)S(1)}, u32[]{:S(2)}, u32[]{:S(2)}) async-start(f32[8,32,128]{2,1,0:T(8,128)} %copy.40), calls=%async_computation | async-start | bytes 262144 | tf_op jit(solution)/shard_map/all_to_all | solution.py:173
  112.0 4.5 %all-to-all-done = f32[8,32,128]{2,1,0:T(8,128)S(1)} async-done(((f32[8,32,128]{2,1,0:T(8,128)}), f32[8,32,128]{2,1,0:T(8,128)S(1)}, u32[]{:S(2)}, u32[]{:S(2)}) %all-to-all-start) | async-done | bytes 131104 | tf_op jit(solution)/shard_map/all_to_all | solution.py:173
  117.3 1.5 %scatter_fusion.1 = f32[4,64,128]{2,0,1:T(4,128)S(1)} fusion(f32[4,64,128]{2,0,1:T(4,128)S(1)} %bitcast.81, s32[32]{0:T(128)S(1)} %multiply_bitcast_fusion.10, f32[32,4,128]{2,1,0:T(4,128)S(1)} %copy.44), kind=kCustom, calls=%fused_computation.1 | custom fusion | bytes 196736 | tf_op jit(solution)/shard_map/scatter | solution.py:117
  119.0 1.0 scatter_fusion.2
  (159 shorter events, 11.1 us)
Async XLA Ops:
  0.6 16.1 %copy-start = (f32[16,64,256]{2,1,0:T(8,128)S(1)}, f32[16,64,256]{2,1,0:T(8,128)}, u32[]{:S(2)}) copy-start(f32[16,64,256]{2,1,0:T(8,128)} %param.9) | copy-start | bytes 3145732
  0.6 16.1 %copy-start.1 = (f32[16,64,256]{2,1,0:T(8,128)S(1)}, f32[16,64,256]{2,1,0:T(8,128)}, u32[]{:S(2)}) copy-start(f32[16,64,256]{2,1,0:T(8,128)} %param.11) | copy-start | bytes 3145732
  2.6 18.4 %collective-permute-start.2 = (f32[4,64,256]{2,1,0:T(8,128)}, f32[4,64,256]{2,1,0:T(8,128)S(1)}, u32[]{:S(2)}, u32[]{:S(2)}) collective-permute-start(f32[4,64,256]{2,1,0:T(8,128)} %get-tuple-element.56), channel_id=1, source_target_pairs={{0,2},{2,4},{4,6},{6,8},{8,10},{10,12},{12,14},{14,16},{16,18},{18... | collective-permute-start | bytes 786440 | tf_op jit(solution)/shard_map/ppermute | solution.py:22
  6.4 16.0 %collective-permute-start.1 = (f32[4,64,256]{2,1,0:T(8,128)}, f32[4,64,256]{2,1,0:T(8,128)S(1)}, u32[]{:S(2)}, u32[]{:S(2)}) collective-permute-start(f32[4,64,256]{2,1,0:T(8,128)} %get-tuple-element.55), channel_id=1, source_target_pairs={{2,0},{4,2},{6,4},{8,6},{10,8},{12,10},{14,12},{16,14},{18,16},{20... | collective-permute-start | bytes 786440 | tf_op jit(solution)/shard_map/ppermute | solution.py:24
  10.2 12.2 %collective-permute-start = (f32[4,64,256]{2,1,0:T(8,128)}, f32[4,64,256]{2,1,0:T(8,128)S(1)}, u32[]{:S(2)}, u32[]{:S(2)}) collective-permute-start(f32[4,64,256]{2,1,0:T(8,128)} %get-tuple-element.53), channel_id=1, source_target_pairs={{2,0},{4,2},{6,4},{8,6},{10,8},{12,10},{14,12},{16,14},{18,16},{20... | collective-permute-start | bytes 786440 | tf_op jit(solution)/shard_map/ppermute | solution.py:24
  12.7 8.5 %collective-permute-start.5 = (f32[4,64,256]{2,1,0:T(8,128)}, f32[4,64,256]{2,1,0:T(8,128)}, u32[]{:S(2)}, u32[]{:S(2)}) collective-permute-start(f32[4,64,256]{2,1,0:T(8,128)} %get-tuple-element.54), channel_id=1, source_target_pairs={{0,2},{2,4},{4,6},{6,8},{8,10},{10,12},{12,14},{14,16},{16,18},{18... | collective-permute-start | bytes 786440 | tf_op jit(solution)/shard_map/ppermute | solution.py:22
  22.1 1.2 %copy-start.2 = (f32[16,64,256]{2,1,0:T(8,128)S(1)}, f32[16,64,256]{2,1,0:T(8,128)}, u32[]{:S(2)}) copy-start(f32[16,64,256]{2,1,0:T(8,128)} %param.11) | copy-start | bytes 3145732
  24.0 15.9 %copy-start.3 = (f32[16,64,256]{2,1,0:T(8,128)}, f32[16,64,256]{2,1,0:T(8,128)S(1)}, u32[]{:S(2)}) copy-start(f32[16,64,256]{2,1,0:T(8,128)S(1)} %get-tuple-element.48) | copy-start | bytes 3145732
  24.1 13.6 %collective-permute-start.7 = (f32[24,4,256]{2,1,0:T(4,128)S(1)}, f32[24,4,256]{2,1,0:T(4,128)S(1)}, u32[]{:S(2)}, u32[]{:S(2)}) collective-permute-start(f32[24,4,256]{2,1,0:T(4,128)S(1)} %get-tuple-element.42), channel_id=1, source_target_pairs={{1,0},{3,2},{5,4},{7,6},{9,8},{11,10},{13,12},{15,14},{17,16},{19,... | collective-permute-start | bytes 294920 | tf_op jit(solution)/shard_map/ppermute | solution.py:24
  25.4 12.3 %collective-permute-start.8 = (f32[24,4,256]{2,1,0:T(4,128)S(1)}, f32[24,4,256]{2,1,0:T(4,128)S(1)}, u32[]{:S(2)}, u32[]{:S(2)}) collective-permute-start(f32[24,4,256]{2,1,0:T(4,128)S(1)} %get-tuple-element.43), channel_id=1, source_target_pairs={{0,1},{2,3},{4,5},{6,7},{8,9},{10,11},{12,13},{14,15},{16,17},{18,... | collective-permute-start | bytes 294920 | tf_op jit(solution)/shard_map/ppermute | solution.py:22
  29.5 8.3 %collective-permute-start.6 = (f32[24,4,256]{2,1,0:T(4,128)S(1)}, f32[24,4,256]{2,1,0:T(4,128)S(1)}, u32[]{:S(2)}, u32[]{:S(2)}) collective-permute-start(f32[24,4,256]{2,1,0:T(4,128)S(1)} %slice.723), channel_id=1, source_target_pairs={{1,0},{3,2},{5,4},{7,6},{9,8},{11,10},{13,12},{15,14},{17,16},{19,... | collective-permute-start | bytes 294920 | tf_op jit(solution)/shard_map/ppermute | solution.py:24
  30.8 17.4 %collective-permute-start.3 = (f32[4,64,256]{2,1,0:T(8,128)S(1)}, f32[4,64,256]{2,1,0:T(8,128)S(1)}, u32[]{:S(2)}, u32[]{:S(2)}) collective-permute-start(f32[4,64,256]{2,1,0:T(8,128)S(1)} %get-tuple-element.44), channel_id=1, source_target_pairs={{0,2},{2,4},{4,6},{6,8},{8,10},{10,12},{12,14},{14,16},{16,18},{18... | collective-permute-start | bytes 786440 | tf_op jit(solution)/shard_map/ppermute | solution.py:22
  35.8 10.8 %copy-start.5 = (s32[4]{0:T(128)S(1)}, s32[4]{0:T(128)}, u32[]{:S(2)}) copy-start(s32[4]{0:T(128)} %clamp_shift-left_fusion.1) | copy-start | bytes 52
  35.8 12.4 %collective-permute-start.4 = (f32[4,64,256]{2,1,0:T(8,128)S(1)}, f32[4,64,256]{2,1,0:T(8,128)}, u32[]{:S(2)}, u32[]{:S(2)}) collective-permute-start(f32[4,64,256]{2,1,0:T(8,128)S(1)} %get-tuple-element.45), channel_id=1, source_target_pairs={{2,0},{4,2},{6,4},{8,6},{10,8},{12,10},{14,12},{16,14},{18,16},{20... | collective-permute-start | bytes 786440 | tf_op jit(solution)/shard_map/ppermute | solution.py:24
  40.0 1.0 copy-start.4
  41.0 5.7 %collective-permute-start.10 = (f32[16,4,256]{2,1,0:T(4,128)}, f32[16,4,256]{2,1,0:T(4,128)S(1)}, u32[]{:S(2)}, u32[]{:S(2)}) collective-permute-start(f32[16,4,256]{2,1,0:T(4,128)} %get-tuple-element.47), channel_id=1, source_target_pairs={{1,0},{3,2},{5,4},{7,6},{9,8},{11,10},{13,12},{15,14},{17,16},{19,... | collective-permute-start | bytes 196616 | tf_op jit(solution)/shard_map/ppermute | solution.py:24
  42.3 5.9 %collective-permute-start.9 = (f32[16,4,256]{2,1,0:T(4,128)}, f32[16,4,256]{2,1,0:T(4,128)S(1)}, u32[]{:S(2)}, u32[]{:S(2)}) collective-permute-start(f32[16,4,256]{2,1,0:T(4,128)} %get-tuple-element.46), channel_id=1, source_target_pairs={{0,1},{2,3},{4,5},{6,7},{8,9},{10,11},{12,13},{14,15},{16,17},{18,... | collective-permute-start | bytes 196616 | tf_op jit(solution)/shard_map/ppermute | solution.py:22
  66.2 7.3 %collective-permute-start.11 = (f32[4,32,128]{2,1,0:T(8,128)S(1)}, f32[4,32,128]{2,1,0:T(8,128)S(1)}, u32[]{:S(2)}, u32[]{:S(2)}) collective-permute-start(f32[4,32,128]{2,1,0:T(8,128)S(1)} %get-tuple-element.68), channel_id=1, source_target_pairs={{0,2},{2,4},{4,6},{6,8},{8,10},{10,12},{12,14},{14,16},{16,18},{18... | collective-permute-start | bytes 196616 | tf_op jit(solution)/shard_map/ppermute | solution.py:22
  71.6 6.5 %collective-permute-start.12 = (f32[4,32,128]{2,1,0:T(8,128)S(1)}, f32[4,32,128]{2,1,0:T(8,128)S(1)}, u32[]{:S(2)}, u32[]{:S(2)}) collective-permute-start(f32[4,32,128]{2,1,0:T(8,128)S(1)} %get-tuple-element.66), channel_id=1, source_target_pairs={{2,0},{4,2},{6,4},{8,6},{10,8},{12,10},{14,12},{16,14},{18,16},{20... | collective-permute-start | bytes 196616 | tf_op jit(solution)/shard_map/ppermute | solution.py:24
  84.3 7.3 %collective-permute-start.13 = (f32[4,32,64]{1,2,0:T(8,128)S(1)}, f32[4,32,64]{1,2,0:T(8,128)S(1)}, u32[]{:S(2)}, u32[]{:S(2)}) collective-permute-start(f32[4,32,64]{1,2,0:T(8,128)S(1)} %slice.632), channel_id=1, source_target_pairs={{2,0},{4,2},{6,4},{8,6},{10,8},{12,10},{14,12},{16,14},{18,16},{20... | collective-permute-start | bytes 98312 | tf_op jit(solution)/shard_map/ppermute | solution.py:24
  86.4 6.5 %collective-permute-start.14 = (f32[4,32,64]{1,2,0:T(8,128)S(1)}, f32[4,32,64]{1,2,0:T(8,128)S(1)}, u32[]{:S(2)}, u32[]{:S(2)}) collective-permute-start(f32[4,32,64]{1,2,0:T(8,128)S(1)} %slice.632), channel_id=1, source_target_pairs={{0,2},{2,4},{4,6},{6,8},{8,10},{10,12},{12,14},{14,16},{16,18},{18... | collective-permute-start | bytes 98312 | tf_op jit(solution)/shard_map/ppermute | solution.py:22
  108.6 7.9 %all-to-all-start = ((f32[8,32,128]{2,1,0:T(8,128)}), f32[8,32,128]{2,1,0:T(8,128)S(1)}, u32[]{:S(2)}, u32[]{:S(2)}) async-start(f32[8,32,128]{2,1,0:T(8,128)} %copy.40), calls=%async_computation | async-start | bytes 262144 | tf_op jit(solution)/shard_map/all_to_all | solution.py:173
where the time goes:
time: 124 us; the launch traced here: 122 us
  starting transfers between devices  48.4 us (39%)
  local copies, waits for them, and re-layouts  38.9 us (31%)
  other arithmetic  20.1 us (16%)
  waiting for transfers between devices  12.4 us (10%)
  between operations  1.88 us (2%)
    ppermute x7, starting transfers between devices, padded_2(): lax.ppermute(tail, axis, [(i, (i + 1) % count) for i in range(ends)])  31 us
    ppermute x8, starting transfers between devices, padded_2(): lax.ppermute(head, axis, [((i + 1) % count, i) for i in range(ends)])  14 us
    scatter x2, local copies, waits for them, and re-layouts, on_device(): planar = planar.at[::2, :, ::2].set(corner)  13.3 us
    add x1, other arithmetic, on_device(): next_field = 2.0 * current - previous + stiffness * laplace_sum  11.3 us
    slice x1, local copies, waits for them, and re-layouts, on_device(): snapshot = next_field[::2, ::2, ::2]  6.72 us
    select_n x3, other arithmetic, compute_flux(): return jnp.where(inside, face_buoy * gradient, jnp.float32(0.0))  6.7 us
    ppermute x8, waiting for transfers between devices, padded_2(): lax.ppermute(head, axis, [((i + 1) % count, i) for i in range(ends)])  5.09 us
    all_to_all x1, waiting for transfers between devices, on_device(): lax.all_to_all(planar, 'gz', split_axis=0, concat_axis=1, tiled=True)  4.54 us
  transfers between devices with their start and end apart: 16, of which 5 were waited for; matrix products, arithmetic and copies ran while one was open for 9% of the time, Pallas kernels for 0%

commit v1 on v0

v1 whole, which is shorter than its diff:
```python
import functools

import jax
import jax.numpy as jnp
import numpy as np
from jax import lax
from jax.experimental import pallas as pl
from jax.experimental.pallas import tpu as pltpu
from jax.sharding import PartitionSpec as P

coeffs = (1225.0 / 1024.0, -245.0 / 3072.0, 49.0 / 5120.0, -5.0 / 7168.0)
alpha_lift = -1.586134342
beta_lift = -0.05298011854
gamma_lift = 0.8829110762
delta_lift = 0.4435068522
wavelet_scale = 1.149604398

UP_ROWS = (0, 2, 4, 6, 1)
DOWN_ROWS = (0, 2, 4, 6, 5, 7)
UP2_ROWS = (0,)
DOWN2_ROWS = (4, 6)
CHUNK = 16
HALO = 8
HIGHEST = lax.Precision.HIGHEST


def lift_rows(v):
    s, d = v[0::2].copy(), v[1::2].copy()
    nxt = lambda a: np.concatenate([a[1:], a[-1:]])
    prv = lambda a: np.concatenate([a[:1], a[:-1]])
    d = d + alpha_lift * (s + nxt(s))
    s = s + beta_lift * (prv(d) + d)
    d = d + gamma_lift * (s + nxt(s))
    s = s + delta_lift * (prv(d) + d)
    out = np.empty_like(v)
    out[0::2], out[1::2] = s * wavelet_scale, d / wavelet_scale
    return out


def two_level(n):
    one = lift_rows(np.eye(n))
    two = one.copy()
    two[0::2] = lift_rows(one[0::2])
    return one, two


def x_table(strips, rows):
    one, two = two_level(strips * rows)
    table = []
    for at in (0, 1, 2, strips - 2, strips - 1):
        entry = []
        for step, wanted in ((0, range(rows)), (1, UP_ROWS), (-1, DOWN_ROWS), (2, UP2_ROWS), (-2, DOWN2_ROWS)):
            for row in wanted:
                to = (at + step) * rows + row
                inside = 0 <= at + step < strips
                for source in range(at * rows, (at + 1) * rows):
                    entry += [two[to, source], one[to, source]] if inside else [0.0, 0.0]
        table.append(entry)
    return np.asarray(table, np.float32)


def y_matrices(n):
    grad = np.zeros((n, n))
    div = np.zeros((n, n))
    for k, c in enumerate(coeffs, 1):
        for j in range(n - 1):
            if j + k < n:
                grad[j + k, j] += c
            if j + 1 - k >= 0:
                grad[j + 1 - k, j] -= c
        for i in range(n):
            if i + k - 1 <= n - 2:
                div[i + k - 1, i] += c
            if i - k >= 0:
                div[i - k, i] -= c
    one, two = two_level(n // 2)
    two[1::2] = one[1::2]
    lift = np.zeros((n, n))
    lift[0::2, : n // 2] = one.T
    lift[0::2, n // 2 :] = two.T
    return grad.astype(np.float32), div.astype(np.float32), lift.astype(np.float32)


def z_matrix(n):
    w = np.eye(n)
    for level in range(4):
        w[:: 2**level] = lift_rows(w[:: 2**level])
    return w.astype(np.float32)


def kernel(
    strips, slabs,
    cur, prev, stiff, buoy, tab, gy, dy, ly, wz,
    next_out, coef_out,
    cp, bp, fx, acc, pv, sv, nf, gv, dv, lv, wv, con, up, down, up2, down2, zfull,
    lsem, ssem, rsem, zssem, zrsem, gssem, grsem,
):
    p, g = lax.axis_index("xy"), lax.axis_index("gz")
    X, Z, Y = cur.shape
    NC = Z // CHUNK
    HX, HC = X // 2, CHUNK // 2
    part = HX // slabs
    has_l, has_r = p > 0, p < strips - 1
    has_ll, has_rr = p > 1, p < strips - 2
    has_b, has_t = g > 0, g < slabs - 1
    near = ((has_l, p - 1), (has_r, p + 1), (has_ll, p - 2), (has_rr, p + 2))

    def local(src, dst, k):
        return pltpu.make_async_copy(src, dst, lsem.at[k])

    body = pl.ds(HALO, Z)
    loads = [
        local(cur, cp.at[pl.ds(3, X), body], 0),
        local(buoy, bp.at[pl.ds(0, X), body], 1),
        local(gy, gv, 2),
        local(dy, dv, 3),
        local(prev, pv, 4),
        local(stiff, sv, 5),
        local(ly, lv, 6),
        local(wz, wv, 7),
    ]
    for c in loads:
        c.start()

    barrier = pltpu.get_barrier_semaphore()
    for there, q in near:
        @pl.when(there)
        def _():
            pl.semaphore_signal(barrier, inc=1, device_id=(q, g), device_id_type=pl.DeviceIdType.MESH)
    for o in range(1, slabs):
        pl.semaphore_signal(
            barrier, inc=1, device_id=(p, lax.rem(g + o, slabs)), device_id_type=pl.DeviceIdType.MESH
        )

    def zero(ref):
        ref[...] = jnp.zeros(ref.shape, jnp.float32)

    @pl.when(jnp.logical_not(has_l))
    def _():
        zero(cp.at[pl.ds(0, 3), body])
        zero(fx.at[pl.ds(0, 4)])
        zero(up)

    @pl.when(jnp.logical_not(has_r))
    def _():
        zero(cp.at[pl.ds(X + 3, 4), body])
        zero(fx.at[pl.ds(X + 4, 3)])
        zero(down)

    @pl.when(jnp.logical_not(has_ll))
    def _():
        zero(up2)

    @pl.when(jnp.logical_not(has_rr))
    def _():
        zero(down2)

    @pl.when(jnp.logical_not(has_b))
    def _():
        zero(cp.at[pl.ds(3, X), pl.ds(0, HALO)])

    @pl.when(jnp.logical_not(has_t))
    def _():
        zero(cp.at[pl.ds(3, X), pl.ds(HALO + Z, HALO)])

    one = lambda there: there.astype(jnp.int32)
    pl.semaphore_wait(barrier, one(has_l) + one(has_r) + one(has_ll) + one(has_rr) + slabs - 1)

    def remote(src, dst, ss, rs, dev):
        return pltpu.make_async_remote_copy(
            src_ref=src, dst_ref=dst, send_sem=ss, recv_sem=rs, device_id=dev,
            device_id_type=pl.DeviceIdType.MESH,
        )

    def x_copy(kind, c):
        z = pl.ds(c * CHUNK, CHUNK)
        zp = pl.ds(HALO + c * CHUNK, CHUNK)
        sends, q, receives, src, dst = (
            (has_l, p - 1, has_r, cur.at[pl.ds(0, 4), z], cp.at[pl.ds(X + 3, 4), zp]),
            (has_r, p + 1, has_l, cur.at[pl.ds(X - 3, 3), z], cp.at[pl.ds(0, 3), zp]),
            (has_l, p - 1, has_r, buoy.at[pl.ds(0, 1), z], bp.at[pl.ds(X, 1), zp]),
            (has_r, p + 1, has_l, fx.at[pl.ds(X, 4), z], fx.at[pl.ds(0, 4), z]),
            (has_l, p - 1, has_r, fx.at[pl.ds(4, 3), z], fx.at[pl.ds(X + 4, 3), z]),
            (has_r, p + 1, has_l, con.at[c, pl.ds(HX, 5)], up.at[c]),
            (has_l, p - 1, has_r, con.at[c, pl.ds(HX + 5, 6)], down.at[c]),
            (has_rr, p + 2, has_ll, con.at[c, pl.ds(HX + 11, 1)], up2.at[c]),
            (has_ll, p - 2, has_rr, con.at[c, pl.ds(HX + 12, 2)], down2.at[c]),
        )[kind]
        return sends, receives, remote(src, dst, ssem.at[kind, c], rsem.at[kind, c], (q, g))

    def z_copy(kind):
        low, high = pl.ds(0, HALO), pl.ds(Z - HALO, HALO)
        below, above = pl.ds(0, HALO), pl.ds(HALO + Z, HALO)
        sends, q, receives, src, dst = (
            (has_b, g - 1, has_t, cur.at[:, low], cp.at[pl.ds(3, X), above]),
            (has_t, g + 1, has_b, cur.at[:, high], cp.at[pl.ds(3, X), below]),
            (has_b, g - 1, has_t, buoy.at[:, low], bp.at[pl.ds(0, X), above]),
            (has_t, g + 1, has_b, buoy.at[:, high], bp.at[pl.ds(0, X), below]),
        )[kind]
        return sends, receives, remote(src, dst, zssem.at[kind], zrsem.at[kind], (p, q))

    def start(copy):
        sends, _, c = copy
        pl.when(sends)(c.start)

    def arrive(copy):
        _, receives, c = copy
        pl.when(receives)(c.wait_recv)

    def sent(copy):
        sends, _, c = copy
        pl.when(sends)(c.wait_send)

    for c in range(NC):
        for kind in (0, 1, 2):
            start(x_copy(kind, c))
        if c == 0:
            for kind in range(4):
                start(z_copy(kind))

    for c in loads[:4]:
        c.wait()

    rows = 4

    def y_part(i, _):
        x = i * rows
        v = cp[pl.ds(x + 3, rows), HALO : HALO + Z, :].reshape(rows * Z, Y)
        b = bp[pl.ds(x, rows), HALO : HALO + Z, :].reshape(rows * Z, Y)
        grad = jnp.dot(v, gv[...], precision=HIGHEST, preferred_element_type=jnp.float32)
        flux = 0.5 * (b + pltpu.roll(b, Y - 1, 1)) * grad
        acc[pl.ds(x, rows)] = jnp.dot(
            flux, dv[...], precision=HIGHEST, preferred_element_type=jnp.float32
        ).reshape(rows, Z, Y)
        return 0

    lax.fori_loop(0, X // rows, y_part, 0)

    for c in range(NC):
        for kind in (0, 1, 2):
            arrive(x_copy(kind, c))
        zp = slice(HALO + c * CHUNK, HALO + (c + 1) * CHUNK)
        z = slice(c * CHUNK, (c + 1) * CHUNK)

        def x_flux(x, _):
            grad = None
            for k, w in enumerate(coeffs, 1):
                term = w * (cp[x + 3 + k, zp, :] - cp[x + 4 - k, zp, :])
                grad = term if grad is None else grad + term
            flux = 0.5 * (bp[x, zp, :] + bp[x + 1, zp, :]) * grad
            keep = jnp.logical_or(has_r, x < X - 1)
            fx[x + 4, z, :] = jnp.where(keep, flux, 0.0)
            return 0

        lax.fori_loop(0, X, x_flux, 0)
        start(x_copy(3, c))
        start(x_copy(4, c))

    for kind in range(4):
        arrive(z_copy(kind))
    ZP = Z + 2 * HALO
    face = lax.broadcasted_iota(jnp.int32, (ZP, Y), 0) - HALO + g * Z
    inside = jnp.logical_and(face >= 0, face <= slabs * Z - 2)

    def moved(v, k):
        return pltpu.roll(v, (-k) % ZP, 0) if k else v

    def z_part(x, _):
        v, b = cp[x + 3], bp[x]
        grad = None
        for k, w in enumerate(coeffs, 1):
            term = w * (moved(v, k) - moved(v, 1 - k))
            grad = term if grad is None else grad + term
        flux = jnp.where(inside, 0.5 * (b + moved(b, 1)) * grad, 0.0)
        div = None
        for k, w in enumerate(coeffs, 1):
            term = w * (moved(flux, k - 1) - moved(flux, -k))
            div = term if div is None else div + term
        acc[x] = acc[x] + div[HALO : HALO + Z]
        return 0

    lax.fori_loop(0, X, z_part, 0)
    for c in loads[4:7]:
        c.wait()

    even = lax.rem(lax.broadcasted_iota(jnp.int32, (HC, Y // 2), 1), 2) == 0
    kind_of = jnp.minimum(p, 2) + jnp.maximum(p - (strips - 3), 0)
    sent_rows = tuple(range(HX)) + UP_ROWS + DOWN_ROWS + UP2_ROWS + DOWN2_ROWS
    stores = []
    for c in range(NC):
        arrive(x_copy(3, c))
        arrive(x_copy(4, c))
        zp = slice(HALO + c * CHUNK, HALO + (c + 1) * CHUNK)
        z = slice(c * CHUNK, (c + 1) * CHUNK)

        def finish(x, _):
            div = None
            for k, w in enumerate(coeffs, 1):
                term = w * (fx[x + 3 + k, z, :] - fx[x + 4 - k, z, :])
                div = term if div is None else div + term
            value = 2.0 * cp[x + 3, zp, :] - pv[x, z, :] + sv[x, z, :] * (div + acc[x, z, :])
            for h in range(Y // 128):
                nf[h, x, z, :] = value[:, h * 128 : (h + 1) * 128]
            return 0

        lax.fori_loop(0, X, finish, 0)
        for h in range(Y // 128):
            zc = pl.ds(c * CHUNK, CHUNK)
            copy = local(nf.at[h, :, zc], next_out.at[:, zc, pl.ds(h * 128, 128)], 8 + 2 * c + h)
            copy.start()
            stores.append(copy)
        snap = jnp.concatenate(
            [
                jnp.concatenate(
                    [nf[h, 2 * r, pl.ds(c * CHUNK, HC, stride=2), :] for h in range(Y // 128)], axis=1
                )
                for r in range(HX)
            ],
            axis=0,
        )
        t = jnp.dot(snap, lv[...], precision=HIGHEST, preferred_element_type=jnp.float32)
        one_y = [t[r * HC : (r + 1) * HC, : Y // 2] for r in range(HX)]
        two_y = [t[r * HC : (r + 1) * HC, Y // 2 :] for r in range(HX)]
        for at, row in enumerate(sent_rows):
            total = None
            for r in range(HX):
                w2 = tab[kind_of, (at * HX + r) * 2]
                w1 = tab[kind_of, (at * HX + r) * 2 + 1]
                term = jnp.where(even, w2, w1) * two_y[r] if row % 2 == 0 else w1 * one_y[r]
                total = term if total is None else total + term
            con[c, at] = total
        for kind in (5, 6, 7, 8):
            start(x_copy(kind, c))

    def g_copy(o, c):
        to = lax.rem(g + o, slabs)
        mine = pl.ds(pl.multiple_of(g * (Z // 2) + c * HC, HC), HC)
        return remote(
            con.at[c, pl.ds(to * part, part)], zfull.at[:, mine],
            gssem.at[o - 1, c], grsem.at[o - 1, c], (p, to),
        )

    for c in range(NC):
        for kind in (5, 6, 7, 8):
            arrive(x_copy(kind, c))
        for row in range(HX):
            total = con[c, row]
            for ref, wanted in ((up, UP_ROWS), (down, DOWN_ROWS), (up2, UP2_ROWS), (down2, DOWN2_ROWS)):
                if row in wanted:
                    total = total + ref[c, wanted.index(row)]
            con[c, row] = total
        for o in range(1, slabs):
            g_copy(o, c).start()
        zfull[:, pl.ds(pl.multiple_of(g * (Z // 2) + c * HC, HC), HC), :] = con[c, pl.ds(g * part, part)]

    loads[7].wait()
    for c in range(NC):
        for o in range(1, slabs):
            g_copy(o, c).wait_recv()
    for row in range(part):
        coef_out[row] = jnp.dot(
            wv[...], zfull[row], precision=HIGHEST, preferred_element_type=jnp.float32
        )

    for copy in stores:
        copy.wait()
    for kind in range(4):
        sent(z_copy(kind))
    for c in range(NC):
        for kind in range(9):
            sent(x_copy(kind, c))
        for o in range(1, slabs):
            g_copy(o, c).wait_send()


def on_device(strips, slabs, previous, current, stiffness, buoyancy):
    X, Z, Y = current.shape
    NC, HX, HC = Z // CHUNK, X // 2, CHUNK // 2
    depth = slabs * Z // 2
    grad, div, lift = y_matrices(Y)
    hbm = pl.BlockSpec(memory_space=pl.ANY)
    f32 = jnp.float32
    vmem = lambda *shape: pltpu.VMEM(shape, f32)
    dma = lambda *shape: pltpu.SemaphoreType.DMA(shape)
    return pl.pallas_call(
        functools.partial(kernel, strips, slabs),
        out_shape=(
            jax.ShapeDtypeStruct((X, Z, Y), f32),
            jax.ShapeDtypeStruct((HX // slabs, depth, Y // 2), f32),
        ),
        in_specs=[hbm] * 4 + [pl.BlockSpec(memory_space=pltpu.SMEM)] + [hbm] * 4,
        out_specs=(hbm, pl.BlockSpec(memory_space=pltpu.VMEM)),
        scratch_shapes=[
            vmem(X + 7, Z + 2 * HALO, Y),
            vmem(X + 1, Z + 2 * HALO, Y),
            vmem(X + 7, Z, Y),
            vmem(X, Z, Y),
            vmem(X, Z, Y),
            vmem(X, Z, Y),
            vmem(Y // 128, X, Z, 128),
            vmem(Y, Y),
            vmem(Y, Y),
            vmem(Y, Y),
            vmem(depth, depth),
            vmem(NC, HX + 14, HC, Y // 2),
            vmem(NC, 5, HC, Y // 2),
            vmem(NC, 6, HC, Y // 2),
            vmem(NC, 1, HC, Y // 2),
            vmem(NC, 2, HC, Y // 2),
            vmem(HX // slabs, depth, Y // 2),
            dma(8 + 2 * NC),
            dma(9, NC),
            dma(9, NC),
            dma(4),
            dma(4),
            dma(slabs - 1, NC),
            dma(slabs - 1, NC),
        ],
        compiler_params=pltpu.CompilerParams(
            collective_id=0, has_side_effects=True, vmem_limit_bytes=40 * 1024 * 1024
        ),
    )(
        current, previous, stiffness, buoyancy,
        x_table(strips, HX), grad, div, lift, z_matrix(depth),
    )


def solution(mesh):
    return jax.shard_map(
        functools.partial(on_device, mesh.shape["xy"], mesh.shape["gz"]),
        mesh=mesh,
        in_specs=(P("xy", "gz", None),) * 4,
        out_specs=(P("xy", "gz", None), P(("xy", "gz"), None, None)),
        check_vma=False,
    )
```

time: 124 us -> 38 us (0.31); the launches traced: 122 us -> 37.5 us
  starting transfers between devices: 48.4 us -> 0 us
  local copies, waits for them, and re-layouts: 38.9 us -> 10.8 us
  Pallas kernels: 0 us -> 26 us
  other arithmetic: 20.1 us -> 0 us
  waiting for transfers between devices: 12.4 us -> 0 us
    ppermute x15 -> x0, starting transfers between devices: 45.1 us -> none  [the longest x7 31 us: padded_2(): lax.ppermute(tail, axis, [(i, (i + 1) % count) for i in range(ends)])]
    pallas_call x0 -> x1, Pallas kernels: none -> 26 us  [on_device(): pl.pallas_call(functools.partial(kernel, strips, slabs), out_shape=(jax.S...]
    slice x61 -> x0, local copies, waits for them, and re-layouts: 18.4 us -> none  [the longest x1 6.72 us: on_device(): snapshot = next_field[::2, ::2, ::2]]
    scatter x5 -> x0, local copies, waits for them, and re-layouts: 16.5 us -> none  [the longest x2 13.3 us: on_device(): planar = planar.at[::2, :, ::2].set(corner)]
    add x19 -> x0, other arithmetic: 11.9 us -> none  [the longest x1 11.3 us: on_device(): next_field = 2.0 * current - previous + stiffness * laplace_sum]
    ppermute x15 -> x0, waiting for transfers between devices: 7.82 us -> none  [the longest x8 5.09 us: padded_2(): lax.ppermute(head, axis, [((i + 1) % count, i) for i in range(ends)])]
    unnamed x16 -> x20, local copies, waits for them, and re-layouts: 3.15 us -> 10.8 us
    select_n x7 -> x0, other arithmetic: 6.76 us -> none  [the longest x3 6.7 us: compute_flux(): return jnp.where(inside, face_buoy * gradient, jnp.float32(0.0))]
  transfers between devices with their start and end apart: 16 -> 0, of which waited for: 5 -> 0; matrix products, arithmetic and copies ran while one was open for 9% -> 0% of each run, Pallas kernels for 0% -> 0%
where the time goes in v1:
time: 38 us; the launch traced here: 37.5 us
  Pallas kernels  26 us (68%)
  local copies, waits for them, and re-layouts  10.8 us (28%)
  between operations  0.66 us (2%)
    pallas_call x1, Pallas kernels, on_device(): pl.pallas_call(functools.partial(kernel, strips, slabs), out_shape=(jax.S...  26 us
    unnamed x20, local copies, waits for them, and re-layouts  10.8 us

profile of v1, /device:TPU:11, one launch (start us, length us, event | category | flops | bytes accessed | tf_op | source)
XLA Modules:
  0.0 37.5 jit_solution(1766826579998059229)
XLA Ops:
  0.6 0.0 copy-start
  0.6 1.2 %copy-done = f32[16,64,256]{2,1,0:T(8,128)S(1)} copy-done((f32[16,64,256]{2,1,0:T(8,128)S(1)}, f32[16,64,256]{2,1,0:T(8,128)}, u32[]{:S(2)}) %copy-start) | copy-done | bytes 1048600
  1.9 0.0 copy-start.1
  1.9 1.2 %copy-done.1 = f32[16,64,256]{2,1,0:T(8,128)S(1)} copy-done((f32[16,64,256]{2,1,0:T(8,128)S(1)}, f32[16,64,256]{2,1,0:T(8,128)}, u32[]{:S(2)}) %copy-start.1) | copy-done | bytes 1048600
  3.1 0.0 copy-start.2
  3.1 1.2 %copy-done.2 = f32[16,64,256]{2,1,0:T(8,128)S(1)} copy-done((f32[16,64,256]{2,1,0:T(8,128)S(1)}, f32[16,64,256]{2,1,0:T(8,128)}, u32[]{:S(2)}) %copy-start.2) | copy-done | bytes 1048600
  4.3 0.0 copy-start.3
  4.3 1.2 %copy-done.3 = f32[16,64,256]{2,1,0:T(8,128)S(1)} copy-done((f32[16,64,256]{2,1,0:T(8,128)S(1)}, f32[16,64,256]{2,1,0:T(8,128)}, u32[]{:S(2)}) %copy-start.3) | copy-done | bytes 1048600
  5.5 0.0 copy-start.4
  5.5 0.9 %copy-done.4 = f32[256,256]{1,0:T(8,128)S(1)} copy-done((f32[256,256]{1,0:T(8,128)S(1)}, f32[256,256]{1,0:T(8,128)}, u32[]{:S(2)}) %copy-start.4) | copy-done | bytes 262168
  6.5 0.0 copy-start.5
  6.5 0.9 %copy-done.5 = f32[256,256]{1,0:T(8,128)S(1)} copy-done((f32[256,256]{1,0:T(8,128)S(1)}, f32[256,256]{1,0:T(8,128)}, u32[]{:S(2)}) %copy-start.5) | copy-done | bytes 262168
  7.4 0.0 copy-start.6
  7.4 0.9 %copy-done.6 = f32[256,256]{1,0:T(8,128)S(1)} copy-done((f32[256,256]{1,0:T(8,128)S(1)}, f32[256,256]{1,0:T(8,128)}, u32[]{:S(2)}) %copy-start.6) | copy-done | bytes 262168
  8.4 0.0 copy-start.7
  8.4 0.8 %copy-done.7 = f32[64,64]{1,0:T(8,128)S(1)} copy-done((f32[64,64]{1,0:T(8,128)S(1)}, f32[64,64]{1,0:T(8,128)}, u32[]{:S(2)}) %copy-start.7) | copy-done | bytes 16408
  9.1 0.0 copy-start.8
  9.1 0.7 %copy-done.8 = f32[5,352]{1,0:T(8,128)S(1)} copy-done((f32[5,352]{1,0:T(8,128)S(1)}, f32[5,352]{1,0:T(8,128)}, u32[]{:S(2)}) %copy-start.8) | copy-done | bytes 7064
  9.8 26.0 %shard_map.104 = (f32[16,64,256]{2,1,0:T(8,128)S(1)}, f32[4,64,128]{2,1,0:T(8,128)S(1)}) custom-call(f32[16,64,256]{2,1,0:T(8,128)S(1)} %copy-done, f32[16,64,256]{2,1,0:T(8,128)S(1)} %copy-done.1, f32[16,64,256]{2,1,0:T(8,128)S(1)} %copy-done.2, f32[16,64,256]{2,1,0:T(8,128)S(1)} %copy-done.3, f32[5,352]{1,0:T(8,128)S(1)} %copy-done.8, ...), custom_call_target="tpu_custom_call" | custom-call | tf_op jit(solution)/shard_map/pallas_call | solution.py:385
  35.9 1.0 %copy.13 = f32[16,64,256]{2,1,0:T(8,128)} copy(f32[16,64,256]{2,1,0:T(8,128)S(1)} %get-tuple-element.4) | data formatting | bytes 2097152
  36.9 0.7 %copy.14 = f32[4,64,128]{2,1,0:T(8,128)} copy(f32[4,64,128]{2,1,0:T(8,128)S(1)} %get-tuple-element.5) | data formatting | bytes 262144
Async XLA Ops:
  0.6 1.2 %copy-start = (f32[16,64,256]{2,1,0:T(8,128)S(1)}, f32[16,64,256]{2,1,0:T(8,128)}, u32[]{:S(2)}) copy-start(f32[16,64,256]{2,1,0:T(8,128)} %cur.1) | copy-start | bytes 3145732
  1.9 1.2 %copy-start.1 = (f32[16,64,256]{2,1,0:T(8,128)S(1)}, f32[16,64,256]{2,1,0:T(8,128)}, u32[]{:S(2)}) copy-start(f32[16,64,256]{2,1,0:T(8,128)} %prev.1) | copy-start | bytes 3145732
  3.1 1.2 %copy-start.2 = (f32[16,64,256]{2,1,0:T(8,128)S(1)}, f32[16,64,256]{2,1,0:T(8,128)}, u32[]{:S(2)}) copy-start(f32[16,64,256]{2,1,0:T(8,128)} %stiff.1) | copy-start | bytes 3145732
  4.3 1.2 %copy-start.3 = (f32[16,64,256]{2,1,0:T(8,128)S(1)}, f32[16,64,256]{2,1,0:T(8,128)}, u32[]{:S(2)}) copy-start(f32[16,64,256]{2,1,0:T(8,128)} %buoy.1) | copy-start | bytes 3145732
  5.5 0.9 %copy-start.4 = (f32[256,256]{1,0:T(8,128)S(1)}, f32[256,256]{1,0:T(8,128)}, u32[]{:S(2)}) copy-start(f32[256,256]{1,0:T(8,128)} %constant.13.clone.ly) | copy-start | bytes 786436
  6.5 0.9 %copy-start.5 = (f32[256,256]{1,0:T(8,128)S(1)}, f32[256,256]{1,0:T(8,128)}, u32[]{:S(2)}) copy-start(f32[256,256]{1,0:T(8,128)} %constant.12.clone.dy) | copy-start | bytes 786436
  7.4 0.9 %copy-start.6 = (f32[256,256]{1,0:T(8,128)S(1)}, f32[256,256]{1,0:T(8,128)}, u32[]{:S(2)}) copy-start(f32[256,256]{1,0:T(8,128)} %constant.11.clone.gy) | copy-start | bytes 786436
  8.4 0.8 %copy-start.7 = (f32[64,64]{1,0:T(8,128)S(1)}, f32[64,64]{1,0:T(8,128)}, u32[]{:S(2)}) copy-start(f32[64,64]{1,0:T(8,128)} %constant.14.clone.wz) | copy-start | bytes 49156
  9.1 0.7 %copy-start.8 = (f32[5,352]{1,0:T(8,128)S(1)}, f32[5,352]{1,0:T(8,128)}, u32[]{:S(2)}) copy-start(f32[5,352]{1,0:T(8,128)} %constant.10.clone.tab) | copy-start | bytes 21124

commit v2 on v1

--- a/solution.py
+++ b/solution.py
@@ -15,10 +15,10 @@
 delta_lift = 0.4435068522
 wavelet_scale = 1.149604398
 
-UP_ROWS = (0, 2, 4, 6, 1)
-DOWN_ROWS = (0, 2, 4, 6, 5, 7)
+UP_ROWS = (0, 2, 1, (4, 6))
+DOWN_ROWS = (4, 6, 5, 7, (0, 2))
 UP2_ROWS = (0,)
-DOWN2_ROWS = (4, 6)
+DOWN2_ROWS = ((4, 6),)
 CHUNK = 16
 HALO = 8
 HIGHEST = lax.Precision.HIGHEST
@@ -44,13 +44,17 @@
     return one, two
 
 
+def flat(rows):
+    return [r for row in rows for r in (row if isinstance(row, tuple) else (row,))]
+
+
 def x_table(strips, rows):
     one, two = two_level(strips * rows)
     table = []
     for at in (0, 1, 2, strips - 2, strips - 1):
         entry = []
         for step, wanted in ((0, range(rows)), (1, UP_ROWS), (-1, DOWN_ROWS), (2, UP2_ROWS), (-2, DOWN2_ROWS)):
-            for row in wanted:
+            for row in flat(wanted):
                 to = (at + step) * rows + row
                 inside = 0 <= at + step < strips
                 for source in range(at * rows, (at + 1) * rows):
@@ -89,10 +93,10 @@
 
 
 def kernel(
-    strips, slabs,
-    cur, prev, stiff, buoy, tab, gy, dy, ly, wz,
+    strips, slabs, used,
+    cur, prev, stiff, buoy, weights, gy, dy, ly, wz,
     next_out, coef_out,
-    cp, bp, fx, acc, pv, sv, nf, gv, dv, lv, wv, con, up, down, up2, down2, zfull,
+    cp, bp, fx, acc, pv, sv, nf, gv, dv, lv, wv, con, up, down, up2, down2, zfull, tab,
     lsem, ssem, rsem, zssem, zrsem, gssem, grsem,
 ):
     p, g = lax.axis_index("xy"), lax.axis_index("gz")
@@ -118,6 +122,7 @@
         local(stiff, sv, 5),
         local(ly, lv, 6),
         local(wz, wv, 7),
+        local(weights, tab, 8 + 2 * NC),
     ]
     for c in loads:
         c.start()
@@ -181,10 +186,10 @@
             (has_l, p - 1, has_r, buoy.at[pl.ds(0, 1), z], bp.at[pl.ds(X, 1), zp]),
             (has_r, p + 1, has_l, fx.at[pl.ds(X, 4), z], fx.at[pl.ds(0, 4), z]),
             (has_l, p - 1, has_r, fx.at[pl.ds(4, 3), z], fx.at[pl.ds(X + 4, 3), z]),
-            (has_r, p + 1, has_l, con.at[c, pl.ds(HX, 5)], up.at[c]),
-            (has_l, p - 1, has_r, con.at[c, pl.ds(HX + 5, 6)], down.at[c]),
-            (has_rr, p + 2, has_ll, con.at[c, pl.ds(HX + 11, 1)], up2.at[c]),
-            (has_ll, p - 2, has_rr, con.at[c, pl.ds(HX + 12, 2)], down2.at[c]),
+            (has_r, p + 1, has_l, con.at[c, pl.ds(HX, 4)], up.at[c]),
+            (has_l, p - 1, has_r, con.at[c, pl.ds(HX + 4, 5)], down.at[c]),
+            (has_rr, p + 2, has_ll, con.at[c, pl.ds(HX + 9, 1)], up2.at[c]),
+            (has_ll, p - 2, has_rr, con.at[c, pl.ds(HX + 10, 1)], down2.at[c]),
         )[kind]
         return sends, receives, remote(src, dst, ssem.at[kind, c], rsem.at[kind, c], (q, g))
 
@@ -211,12 +216,17 @@
         sends, _, c = copy
         pl.when(sends)(c.wait_send)
 
-    for c in range(NC):
-        for kind in (0, 1, 2):
-            start(x_copy(kind, c))
-        if c == 0:
-            for kind in range(4):
-                start(z_copy(kind))
+    order = tuple(range(1, NC - 1)) + (0, NC - 1)
+
+    def halo(n):
+        if n < NC:
+            for kind in (0, 1, 2):
+                start(x_copy(kind, order[n]))
+
+    halo(0)
+    for kind in range(4):
+        start(z_copy(kind))
+    halo(1)
 
     for c in loads[:4]:
         c.wait()
@@ -234,9 +244,32 @@
         ).reshape(rows, Z, Y)
         return 0
 
-    lax.fori_loop(0, X // rows, y_part, 0)
-
-    for c in range(NC):
+    def z_part(begin, end, first, last):
+        n = last - first
+        face = lax.broadcasted_iota(jnp.int32, (n, Y), 0) + (first - HALO) + g * Z
+        inside = jnp.logical_and(face >= 0, face <= slabs * Z - 2)
+
+        def moved(v, k):
+            return pltpu.roll(v, (-k) % n, 0) if k else v
+
+        def row(x, _):
+            v, b = cp[x + 3, first:last, :], bp[x, first:last, :]
+            grad = None
+            for k, w in enumerate(coeffs, 1):
+                term = w * (moved(v, k) - moved(v, 1 - k))
+                grad = term if grad is None else grad + term
+            flux = jnp.where(inside, 0.5 * (b + moved(b, 1)) * grad, 0.0)
+            div = None
+            for k, w in enumerate(coeffs, 1):
+                term = w * (moved(flux, k - 1) - moved(flux, -k))
+                div = term if div is None else div + term
+            at = begin + HALO - first
+            acc[x, begin:end, :] = acc[x, begin:end, :] + div[at : at + end - begin]
+            return 0
+
+        lax.fori_loop(0, X, row, 0)
+
+    def flux_part(c):
         for kind in (0, 1, 2):
             arrive(x_copy(kind, c))
         zp = slice(HALO + c * CHUNK, HALO + (c + 1) * CHUNK)
@@ -256,38 +289,12 @@
         start(x_copy(3, c))
         start(x_copy(4, c))
 
-    for kind in range(4):
-        arrive(z_copy(kind))
-    ZP = Z + 2 * HALO
-    face = lax.broadcasted_iota(jnp.int32, (ZP, Y), 0) - HALO + g * Z
-    inside = jnp.logical_and(face >= 0, face <= slabs * Z - 2)
-
-    def moved(v, k):
-        return pltpu.roll(v, (-k) % ZP, 0) if k else v
-
-    def z_part(x, _):
-        v, b = cp[x + 3], bp[x]
-        grad = None
-        for k, w in enumerate(coeffs, 1):
-            term = w * (moved(v, k) - moved(v, 1 - k))
-            grad = term if grad is None else grad + term
-        flux = jnp.where(inside, 0.5 * (b + moved(b, 1)) * grad, 0.0)
-        div = None
-        for k, w in enumerate(coeffs, 1):
-            term = w * (moved(flux, k - 1) - moved(flux, -k))
-            div = term if div is None else div + term
-        acc[x] = acc[x] + div[HALO : HALO + Z]
-        return 0
-
-    lax.fori_loop(0, X, z_part, 0)
-    for c in loads[4:7]:
-        c.wait()
-
     even = lax.rem(lax.broadcasted_iota(jnp.int32, (HC, Y // 2), 1), 2) == 0
     kind_of = jnp.minimum(p, 2) + jnp.maximum(p - (strips - 3), 0)
     sent_rows = tuple(range(HX)) + UP_ROWS + DOWN_ROWS + UP2_ROWS + DOWN2_ROWS
     stores = []
-    for c in range(NC):
+
+    def finish_part(c):
         arrive(x_copy(3, c))
         arrive(x_copy(4, c))
         zp = slice(HALO + c * CHUNK, HALO + (c + 1) * CHUNK)
@@ -321,14 +328,21 @@
         t = jnp.dot(snap, lv[...], precision=HIGHEST, preferred_element_type=jnp.float32)
         one_y = [t[r * HC : (r + 1) * HC, : Y // 2] for r in range(HX)]
         two_y = [t[r * HC : (r + 1) * HC, Y // 2 :] for r in range(HX)]
-        for at, row in enumerate(sent_rows):
-            total = None
-            for r in range(HX):
-                w2 = tab[kind_of, (at * HX + r) * 2]
-                w1 = tab[kind_of, (at * HX + r) * 2 + 1]
-                term = jnp.where(even, w2, w1) * two_y[r] if row % 2 == 0 else w1 * one_y[r]
-                total = term if total is None else total + term
-            con[c, at] = total
+        at = 0
+        for slot, group in enumerate(sent_rows):
+            totals = []
+            for row in group if isinstance(group, tuple) else (group,):
+                total = None
+                for r in range(HX):
+                    i = at * HX + r
+                    if not used[i]:
+                        continue
+                    w2, w1 = tab[kind_of, 2 * i], tab[kind_of, 2 * i + 1]
+                    term = jnp.where(even, w2, w1) * two_y[r] if row % 2 == 0 else w1 * one_y[r]
+                    total = term if total is None else total + term
+                totals.append(total)
+                at += 1
+            con[c, slot] = totals[0] if len(totals) == 1 else totals[0] + pltpu.roll(totals[1], 1, 1)
         for kind in (5, 6, 7, 8):
             start(x_copy(kind, c))
 
@@ -340,18 +354,48 @@
             gssem.at[o - 1, c], grsem.at[o - 1, c], (p, to),
         )
 
-    for c in range(NC):
+    def planar_part(c):
         for kind in (5, 6, 7, 8):
             arrive(x_copy(kind, c))
+        total = [con[c, row] for row in range(HX)]
+        for ref, wanted in ((up, UP_ROWS), (down, DOWN_ROWS), (up2, UP2_ROWS), (down2, DOWN2_ROWS)):
+            for slot, group in enumerate(wanted):
+                got = ref[c, slot]
+                if isinstance(group, tuple):
+                    total[group[0]] += jnp.where(even, got, 0.0)
+                    total[group[1]] += jnp.where(even, pltpu.roll(got, Y // 2 - 1, 1), 0.0)
+                else:
+                    total[group] += got
         for row in range(HX):
-            total = con[c, row]
-            for ref, wanted in ((up, UP_ROWS), (down, DOWN_ROWS), (up2, UP2_ROWS), (down2, DOWN2_ROWS)):
-                if row in wanted:
-                    total = total + ref[c, wanted.index(row)]
-            con[c, row] = total
+            con[c, row] = total[row]
         for o in range(1, slabs):
             g_copy(o, c).start()
         zfull[:, pl.ds(pl.multiple_of(g * (Z // 2) + c * HC, HC), HC), :] = con[c, pl.ds(g * part, part)]
+
+    blocks = X // rows
+    lax.fori_loop(0, blocks // 2, y_part, 0)
+    flux_part(order[0])
+    halo(2)
+    lax.fori_loop(blocks // 2, blocks, y_part, 0)
+    flux_part(order[1])
+    halo(3)
+    z_part(HALO, Z - HALO, HALO, HALO + Z)
+    for c in loads[4:7] + loads[8:]:
+        c.wait()
+    finish_part(order[0])
+    flux_part(order[2])
+    finish_part(order[1])
+    flux_part(order[3])
+    for kind in range(4):
+        arrive(z_copy(kind))
+    z_part(0, HALO, 0, 3 * HALO)
+    z_part(Z - HALO, Z, Z - HALO, Z + 2 * HALO)
+    finish_part(order[2])
+    planar_part(order[0])
+    finish_part(order[3])
+    planar_part(order[1])
+    planar_part(order[2])
+    planar_part(order[3])
 
     loads[7].wait()
     for c in range(NC):
@@ -373,22 +417,28 @@
             g_copy(o, c).wait_send()
 
 
+def pin(array):
+    return pltpu.with_memory_space_constraint(jnp.asarray(array), pltpu.HBM)
+
+
 def on_device(strips, slabs, previous, current, stiffness, buoyancy):
     X, Z, Y = current.shape
     NC, HX, HC = Z // CHUNK, X // 2, CHUNK // 2
     depth = slabs * Z // 2
     grad, div, lift = y_matrices(Y)
-    hbm = pl.BlockSpec(memory_space=pl.ANY)
+    hbm = pl.BlockSpec(memory_space=pltpu.HBM)
+    table = x_table(strips, HX)
+    used = tuple((table != 0).any(0).reshape(-1, 2).any(1).tolist())
     f32 = jnp.float32
     vmem = lambda *shape: pltpu.VMEM(shape, f32)
     dma = lambda *shape: pltpu.SemaphoreType.DMA(shape)
     return pl.pallas_call(
-        functools.partial(kernel, strips, slabs),
+        functools.partial(kernel, strips, slabs, used),
         out_shape=(
             jax.ShapeDtypeStruct((X, Z, Y), f32),
             jax.ShapeDtypeStruct((HX // slabs, depth, Y // 2), f32),
         ),
-        in_specs=[hbm] * 4 + [pl.BlockSpec(memory_space=pltpu.SMEM)] + [hbm] * 4,
+        in_specs=[hbm] * 9,
         out_specs=(hbm, pl.BlockSpec(memory_space=pltpu.VMEM)),
         scratch_shapes=[
             vmem(X + 7, Z + 2 * HALO, Y),
@@ -402,13 +452,14 @@
             vmem(Y, Y),
             vmem(Y, Y),
             vmem(depth, depth),
-            vmem(NC, HX + 14, HC, Y // 2),
+            vmem(NC, HX + 11, HC, Y // 2),
+            vmem(NC, 4, HC, Y // 2),
             vmem(NC, 5, HC, Y // 2),
-            vmem(NC, 6, HC, Y // 2),
             vmem(NC, 1, HC, Y // 2),
-            vmem(NC, 2, HC, Y // 2),
+            vmem(NC, 1, HC, Y // 2),
             vmem(HX // slabs, depth, Y // 2),
-            dma(8 + 2 * NC),
+            pltpu.SMEM(table.shape, f32),
+            dma(9 + 2 * NC),
             dma(9, NC),
             dma(9, NC),
             dma(4),
@@ -420,8 +471,8 @@
             collective_id=0, has_side_effects=True, vmem_limit_bytes=40 * 1024 * 1024
         ),
     )(
-        current, previous, stiffness, buoyancy,
-        x_table(strips, HX), grad, div, lift, z_matrix(depth),
+        pin(current), pin(previous), pin(stiffness), pin(buoyancy),
+        pin(table), pin(grad), pin(div), pin(lift), pin(z_matrix(depth)),
     )
 
 

time: 38 us -> 28.9 us (0.76)
  the two profiles are of different devices: /device:TPU:11 before, /device:TPU:0 now
where the time goes in v2:
time: 28.9 us; the launch traced here: 28.7 us
  Pallas kernels  26.5 us (92%)
  local copies, waits for them, and re-layouts  1.63 us (6%)
  between operations  0.64 us (2%)
    pallas_call x1, Pallas kernels, on_device(): pl.pallas_call(functools.partial(kernel, strips, slabs, used), out_shape=...  26.5 us
    unnamed x2, local copies, waits for them, and re-layouts  1.63 us

profile of v2, /device:TPU:0, one launch (start us, length us, event | category | flops | bytes accessed | tf_op | source)
XLA Modules:
  0.0 28.7 jit_solution(12729886827010837390)
XLA Ops:
  0.6 26.5 %shard_map.104 = (f32[16,64,256]{2,1,0:T(8,128)S(1)}, f32[4,64,128]{2,1,0:T(8,128)S(1)}) custom-call(f32[16,64,256]{2,1,0:T(8,128)} %cur.1, f32[16,64,256]{2,1,0:T(8,128)} %prev.1, f32[16,64,256]{2,1,0:T(8,128)} %stiff.1, f32[16,64,256]{2,1,0:T(8,128)} %buoy.1, f32[5,352]{1,0:T(8,128)} %constant.10.clone.weights, f32[256,256]{1,0:T(8,128)} %constant.11.clone.gy, ...), custom_call_target="tpu_custom_call" | custom-call | tf_op jit(solution)/shard_map/pallas_call | solution.py:435
  27.1 1.0 %copy.13 = f32[16,64,256]{2,1,0:T(8,128)} copy(f32[16,64,256]{2,1,0:T(8,128)S(1)} %get-tuple-element.4) | data formatting | bytes 2097152
  28.1 0.7 %copy.14 = f32[4,64,128]{2,1,0:T(8,128)} copy(f32[4,64,128]{2,1,0:T(8,128)S(1)} %get-tuple-element.5) | data formatting | bytes 262144

commit v3 on v2

--- a/solution.py
+++ b/solution.py
@@ -15,10 +15,14 @@
 delta_lift = 0.4435068522
 wavelet_scale = 1.149604398
 
-UP_ROWS = (0, 2, 1, (4, 6))
-DOWN_ROWS = (4, 6, 5, 7, (0, 2))
-UP2_ROWS = (0,)
-DOWN2_ROWS = ((4, 6),)
+FLOWS = (
+    (0, (0, 1, 2, 3, 4, 5, 6, 7)),
+    (1, (0, 1, 2, (4, 6))),
+    (-1, (4, 5, 6, 7, (0, 2))),
+    (2, (0,)),
+    (-2, ((4, 6),)),
+)
+SLOTS = tuple(slot for _, slots in FLOWS for slot in slots)
 CHUNK = 16
 HALO = 8
 HIGHEST = lax.Precision.HIGHEST
@@ -44,8 +48,14 @@
     return one, two
 
 
-def flat(rows):
-    return [r for row in rows for r in (row if isinstance(row, tuple) else (row,))]
+def pair(slot):
+    return slot if isinstance(slot, tuple) else (slot,)
+
+
+def owned(slots, owner, part):
+    mine = [i for i, slot in enumerate(slots) if any(row // part == owner for row in pair(slot))]
+    assert mine == list(range(mine[0], mine[0] + len(mine))) if mine else True
+    return (mine[0], len(mine)) if mine else (0, 0)
 
 
 def x_table(strips, rows):
@@ -53,8 +63,8 @@
     table = []
     for at in (0, 1, 2, strips - 2, strips - 1):
         entry = []
-        for step, wanted in ((0, range(rows)), (1, UP_ROWS), (-1, DOWN_ROWS), (2, UP2_ROWS), (-2, DOWN2_ROWS)):
-            for row in flat(wanted):
+        for step, slots in FLOWS:
+            for row in (row for slot in slots for row in pair(slot)):
                 to = (at + step) * rows + row
                 inside = 0 <= at + step < strips
                 for source in range(at * rows, (at + 1) * rows):
@@ -96,8 +106,8 @@
     strips, slabs, used,
     cur, prev, stiff, buoy, weights, gy, dy, ly, wz,
     next_out, coef_out,
-    cp, bp, fx, acc, pv, sv, nf, gv, dv, lv, wv, con, up, down, up2, down2, zfull, tab,
-    lsem, ssem, rsem, zssem, zrsem, gssem, grsem,
+    cp, bp, fx, acc, pv, sv, nf, gv, dv, lv, wv, con, got, zfull, tab,
+    lsem, ssem, rsem, zssem, zrsem, cssem, crsem,
 ):
     p, g = lax.axis_index("xy"), lax.axis_index("gz")
     X, Z, Y = cur.shape
@@ -108,6 +118,7 @@
     has_ll, has_rr = p > 1, p < strips - 2
     has_b, has_t = g > 0, g < slabs - 1
     near = ((has_l, p - 1), (has_r, p + 1), (has_ll, p - 2), (has_rr, p + 2))
+    reach = {0: True, 1: has_r, -1: has_l, 2: has_rr, -2: has_ll}
 
     def local(src, dst, k):
         return pltpu.make_async_copy(src, dst, lsem.at[k])
@@ -131,12 +142,18 @@
     for there, q in near:
         @pl.when(there)
         def _():
-            pl.semaphore_signal(barrier, inc=1, device_id=(q, g), device_id_type=pl.DeviceIdType.MESH)
+            for o in range(slabs):
+                pl.semaphore_signal(barrier, inc=1, device_id=(q, o), device_id_type=pl.DeviceIdType.MESH)
     for o in range(1, slabs):
         pl.semaphore_signal(
             barrier, inc=1, device_id=(p, lax.rem(g + o, slabs)), device_id_type=pl.DeviceIdType.MESH
         )
 
+    room, base = [], []
+    for _, slots in FLOWS:
+        base.append(sum(room))
+        room.append(max(owned(slots, o, part)[1] for o in range(slabs)))
+
     def zero(ref):
         ref[...] = jnp.zeros(ref.shape, jnp.float32)
 
@@ -144,21 +161,21 @@
     def _():
         zero(cp.at[pl.ds(0, 3), body])
         zero(fx.at[pl.ds(0, 4)])
-        zero(up)
+        zero(got.at[:, :, pl.ds(base[1], room[1])])
 
     @pl.when(jnp.logical_not(has_r))
     def _():
         zero(cp.at[pl.ds(X + 3, 4), body])
         zero(fx.at[pl.ds(X + 4, 3)])
-        zero(down)
+        zero(got.at[:, :, pl.ds(base[2], room[2])])
 
     @pl.when(jnp.logical_not(has_ll))
     def _():
-        zero(up2)
+        zero(got.at[:, :, pl.ds(base[3], room[3])])
 
     @pl.when(jnp.logical_not(has_rr))
     def _():
-        zero(down2)
+        zero(got.at[:, :, pl.ds(base[4], room[4])])
 
     @pl.when(jnp.logical_not(has_b))
     def _():
@@ -169,7 +186,7 @@
         zero(cp.at[pl.ds(3, X), pl.ds(HALO + Z, HALO)])
 
     one = lambda there: there.astype(jnp.int32)
-    pl.semaphore_wait(barrier, one(has_l) + one(has_r) + one(has_ll) + one(has_rr) + slabs - 1)
+    pl.semaphore_wait(barrier, slabs * (one(has_l) + one(has_r) + one(has_ll) + one(has_rr)) + slabs - 1)
 
     def remote(src, dst, ss, rs, dev):
         return pltpu.make_async_remote_copy(
@@ -186,10 +203,6 @@
             (has_l, p - 1, has_r, buoy.at[pl.ds(0, 1), z], bp.at[pl.ds(X, 1), zp]),
             (has_r, p + 1, has_l, fx.at[pl.ds(X, 4), z], fx.at[pl.ds(0, 4), z]),
             (has_l, p - 1, has_r, fx.at[pl.ds(4, 3), z], fx.at[pl.ds(X + 4, 3), z]),
-            (has_r, p + 1, has_l, con.at[c, pl.ds(HX, 4)], up.at[c]),
-            (has_l, p - 1, has_r, con.at[c, pl.ds(HX + 4, 5)], down.at[c]),
-            (has_rr, p + 2, has_ll, con.at[c, pl.ds(HX + 9, 1)], up2.at[c]),
-            (has_ll, p - 2, has_rr, con.at[c, pl.ds(HX + 10, 1)], down2.at[c]),
         )[kind]
         return sends, receives, remote(src, dst, ssem.at[kind, c], rsem.at[kind, c], (q, g))
 
@@ -205,14 +218,20 @@
         return sends, receives, remote(src, dst, zssem.at[kind], zrsem.at[kind], (p, q))
 
     def start(copy):
+        if copy is None:
+            return
         sends, _, c = copy
         pl.when(sends)(c.start)
 
     def arrive(copy):
+        if copy is None:
+            return
         _, receives, c = copy
         pl.when(receives)(c.wait_recv)
 
     def sent(copy):
+        if copy is None:
+            return
         sends, _, c = copy
         pl.when(sends)(c.wait_send)
 
@@ -291,7 +310,6 @@
 
     even = lax.rem(lax.broadcasted_iota(jnp.int32, (HC, Y // 2), 1), 2) == 0
     kind_of = jnp.minimum(p, 2) + jnp.maximum(p - (strips - 3), 0)
-    sent_rows = tuple(range(HX)) + UP_ROWS + DOWN_ROWS + UP2_ROWS + DOWN2_ROWS
     stores = []
 
     def finish_part(c):
@@ -329,9 +347,9 @@
         one_y = [t[r * HC : (r + 1) * HC, : Y // 2] for r in range(HX)]
         two_y = [t[r * HC : (r + 1) * HC, Y // 2 :] for r in range(HX)]
         at = 0
-        for slot, group in enumerate(sent_rows):
+        for slot, group in enumerate(SLOTS):
             totals = []
-            for row in group if isinstance(group, tuple) else (group,):
+            for row in pair(group):
                 total = None
                 for r in range(HX):
                     i = at * HX + r
@@ -343,34 +361,52 @@
                 totals.append(total)
                 at += 1
             con[c, slot] = totals[0] if len(totals) == 1 else totals[0] + pltpu.roll(totals[1], 1, 1)
-        for kind in (5, 6, 7, 8):
-            start(x_copy(kind, c))
-
-    def g_copy(o, c):
-        to = lax.rem(g + o, slabs)
-        mine = pl.ds(pl.multiple_of(g * (Z // 2) + c * HC, HC), HC)
-        return remote(
-            con.at[c, pl.ds(to * part, part)], zfull.at[:, mine],
-            gssem.at[o - 1, c], grsem.at[o - 1, c], (p, to),
+        for f in range(len(FLOWS)):
+            for o in range(slabs):
+                start(sum_copy(f, o, None, c))
+        for o in range(slabs):
+            @pl.when(g == o)
+            def _():
+                first, n = owned(FLOWS[0][1], o, part)
+                got[c, o, 0:n] = con[c, first : first + n]
+
+    def sum_copy(f, o, s, c):
+        step, slots = FLOWS[f]
+        first, n = owned(slots, o, part)
+        if not n:
+            return None
+        here = sum(len(slots) for _, slots in FLOWS[:f]) + first
+        copy = remote(
+            con.at[c, pl.ds(here, n)], got.at[c, g if s is None else s, pl.ds(base[f], n)],
+            cssem.at[f, o, c], crsem.at[f, g if s is None else s, c], (p + step, o),
         )
+        return (reach[step] if step else g != o), (reach[-step] if step else g != s), copy
 
     def planar_part(c):
-        for kind in (5, 6, 7, 8):
-            arrive(x_copy(kind, c))
-        total = [con[c, row] for row in range(HX)]
-        for ref, wanted in ((up, UP_ROWS), (down, DOWN_ROWS), (up2, UP2_ROWS), (down2, DOWN2_ROWS)):
-            for slot, group in enumerate(wanted):
-                got = ref[c, slot]
-                if isinstance(group, tuple):
-                    total[group[0]] += jnp.where(even, got, 0.0)
-                    total[group[1]] += jnp.where(even, pltpu.roll(got, Y // 2 - 1, 1), 0.0)
-                else:
-                    total[group] += got
-        for row in range(HX):
-            con[c, row] = total[row]
-        for o in range(1, slabs):
-            g_copy(o, c).start()
-        zfull[:, pl.ds(pl.multiple_of(g * (Z // 2) + c * HC, HC), HC), :] = con[c, pl.ds(g * part, part)]
+        for o in range(slabs):
+            @pl.when(g == o)
+            def _():
+                for s in range(slabs):
+                    total = [None] * part
+                    for f, (_, slots) in enumerate(FLOWS):
+                        arrive(sum_copy(f, o, s, c))
+                    for f, (_, slots) in enumerate(FLOWS):
+                        first, n = owned(slots, o, part)
+                        for i in range(n):
+                            slot = slots[first + i]
+                            value = got[c, s, base[f] + i]
+                            for at, row in enumerate(pair(slot)):
+                                if row // part != o:
+                                    continue
+                                term = value
+                                if isinstance(slot, tuple):
+                                    term = pltpu.roll(value, Y // 2 - 1, 1) if at else value
+                                    term = jnp.where(even, term, 0.0)
+                                k = row - o * part
+                                total[k] = term if total[k] is None else total[k] + term
+                    at = s * (Z // 2) + c * HC
+                    for k in range(part):
+                        zfull[k, at : at + HC, :] = total[k]
 
     blocks = X // rows
     lax.fori_loop(0, blocks // 2, y_part, 0)
@@ -380,12 +416,12 @@
     flux_part(order[1])
     halo(3)
     z_part(HALO, Z - HALO, HALO, HALO + Z)
+    flux_part(order[2])
     for c in loads[4:7] + loads[8:]:
         c.wait()
     finish_part(order[0])
-    flux_part(order[2])
+    flux_part(order[3])
     finish_part(order[1])
-    flux_part(order[3])
     for kind in range(4):
         arrive(z_copy(kind))
     z_part(0, HALO, 0, 3 * HALO)
@@ -393,14 +429,9 @@
     finish_part(order[2])
     planar_part(order[0])
     finish_part(order[3])
-    planar_part(order[1])
-    planar_part(order[2])
-    planar_part(order[3])
-
     loads[7].wait()
-    for c in range(NC):
-        for o in range(1, slabs):
-            g_copy(o, c).wait_recv()
+    for n in range(1, NC):
+        planar_part(order[n])
     for row in range(part):
         coef_out[row] = jnp.dot(
             wv[...], zfull[row], precision=HIGHEST, preferred_element_type=jnp.float32
@@ -411,10 +442,11 @@
     for kind in range(4):
         sent(z_copy(kind))
     for c in range(NC):
-        for kind in range(9):
+        for kind in range(5):
             sent(x_copy(kind, c))
-        for o in range(1, slabs):
-            g_copy(o, c).wait_send()
+        for f in range(len(FLOWS)):
+            for o in range(slabs):
+                sent(sum_copy(f, o, None, c))
 
 
 def pin(array):
@@ -427,6 +459,8 @@
     depth = slabs * Z // 2
     grad, div, lift = y_matrices(Y)
     hbm = pl.BlockSpec(memory_space=pltpu.HBM)
+    part = HX // slabs
+    places = sum(max(owned(slots, o, part)[1] for o in range(slabs)) for _, slots in FLOWS)
     table = x_table(strips, HX)
     used = tuple((table != 0).any(0).reshape(-1, 2).any(1).tolist())
     f32 = jnp.float32
@@ -452,20 +486,17 @@
             vmem(Y, Y),
             vmem(Y, Y),
             vmem(depth, depth),
-            vmem(NC, HX + 11, HC, Y // 2),
-            vmem(NC, 4, HC, Y // 2),
-            vmem(NC, 5, HC, Y // 2),
-            vmem(NC, 1, HC, Y // 2),
-            vmem(NC, 1, HC, Y // 2),
+            vmem(NC, len(SLOTS), HC, Y // 2),
+            vmem(NC, slabs, places, HC, Y // 2),
             vmem(HX // slabs, depth, Y // 2),
             pltpu.SMEM(table.shape, f32),
             dma(9 + 2 * NC),
-            dma(9, NC),
-            dma(9, NC),
+            dma(5, NC),
+            dma(5, NC),
             dma(4),
             dma(4),
-            dma(slabs - 1, NC),
-            dma(slabs - 1, NC),
+            dma(len(FLOWS), slabs, NC),
+            dma(len(FLOWS), slabs, NC),
         ],
         compiler_params=pltpu.CompilerParams(
             collective_id=0, has_side_effects=True, vmem_limit_bytes=40 * 1024 * 1024

time: 28.9 us -> 26.5 us (0.917)
  the two profiles are of different devices: /device:TPU:0 before, /device:TPU:1 now
where the time goes in v3:
time: 26.5 us; the launch traced here: 26.4 us
  Pallas kernels  24.1 us (91%)
  local copies, waits for them, and re-layouts  1.63 us (6%)
  between operations  0.64 us (2%)
    pallas_call x1, Pallas kernels, on_device(): pl.pallas_call(functools.partial(kernel, strips, slabs, used), out_shape=...  24.1 us
    unnamed x2, local copies, waits for them, and re-layouts  1.63 us

profile of v3, /device:TPU:1, one launch (start us, length us, event | category | flops | bytes accessed | tf_op | source)
XLA Modules:
  0.0 26.4 jit_solution(12467310675279424686)
XLA Ops:
  0.6 24.1 %shard_map.104 = (f32[16,64,256]{2,1,0:T(8,128)S(1)}, f32[4,64,128]{2,1,0:T(8,128)S(1)}) custom-call(f32[16,64,256]{2,1,0:T(8,128)} %cur.1, f32[16,64,256]{2,1,0:T(8,128)} %prev.1, f32[16,64,256]{2,1,0:T(8,128)} %stiff.1, f32[16,64,256]{2,1,0:T(8,128)} %buoy.1, f32[5,352]{1,0:T(8,128)} %constant.10.clone.weights, f32[256,256]{1,0:T(8,128)} %constant.11.clone.gy, ...), custom_call_target="tpu_custom_call" | custom-call | tf_op jit(solution)/shard_map/pallas_call | solution.py:469
  24.8 1.0 %copy.13 = f32[16,64,256]{2,1,0:T(8,128)} copy(f32[16,64,256]{2,1,0:T(8,128)S(1)} %get-tuple-element.4) | data formatting | bytes 2097152
  25.7 0.7 %copy.14 = f32[4,64,128]{2,1,0:T(8,128)} copy(f32[4,64,128]{2,1,0:T(8,128)S(1)} %get-tuple-element.5) | data formatting | bytes 262144

commit v4 on v3

--- a/solution.py
+++ b/solution.py
@@ -104,9 +104,9 @@
 
 def kernel(
     strips, slabs, used,
-    cur, prev, stiff, buoy, weights, gy, dy, ly, wz,
-    next_out, coef_out,
-    cp, bp, fx, acc, pv, sv, nf, gv, dv, lv, wv, con, got, zfull, tab,
+    cur, prev, stiff, buoy, weights, gy, dy, ly,
+    next_out, zfull,
+    cp, bp, fx, acc, pv, sv, nf, gv, dv, lv, con, got, tab,
     lsem, ssem, rsem, zssem, zrsem, cssem, crsem,
 ):
     p, g = lax.axis_index("xy"), lax.axis_index("gz")
@@ -132,8 +132,7 @@
         local(prev, pv, 4),
         local(stiff, sv, 5),
         local(ly, lv, 6),
-        local(wz, wv, 7),
-        local(weights, tab, 8 + 2 * NC),
+        local(weights, tab, 7),
     ]
     for c in loads:
         c.start()
@@ -242,10 +241,8 @@
             for kind in (0, 1, 2):
                 start(x_copy(kind, order[n]))
 
-    halo(0)
-    for kind in range(4):
-        start(z_copy(kind))
-    halo(1)
+    for n in range(3):
+        halo(n)
 
     for c in loads[:4]:
         c.wait()
@@ -304,9 +301,11 @@
             fx[x + 4, z, :] = jnp.where(keep, flux, 0.0)
             return 0
 
-        lax.fori_loop(0, X, x_flux, 0)
+        lax.fori_loop(X - 4, X, x_flux, 0)
         start(x_copy(3, c))
+        lax.fori_loop(0, 3, x_flux, 0)
         start(x_copy(4, c))
+        lax.fori_loop(3, X - 4, x_flux, 0)
 
     even = lax.rem(lax.broadcasted_iota(jnp.int32, (HC, Y // 2), 1), 2) == 0
     kind_of = jnp.minimum(p, 2) + jnp.maximum(p - (strips - 3), 0)
@@ -411,13 +410,14 @@
     blocks = X // rows
     lax.fori_loop(0, blocks // 2, y_part, 0)
     flux_part(order[0])
-    halo(2)
+    halo(3)
+    for kind in range(4):
+        start(z_copy(kind))
     lax.fori_loop(blocks // 2, blocks, y_part, 0)
     flux_part(order[1])
-    halo(3)
     z_part(HALO, Z - HALO, HALO, HALO + Z)
     flux_part(order[2])
-    for c in loads[4:7] + loads[8:]:
+    for c in loads[4:]:
         c.wait()
     finish_part(order[0])
     flux_part(order[3])
@@ -429,14 +429,8 @@
     finish_part(order[2])
     planar_part(order[0])
     finish_part(order[3])
-    loads[7].wait()
     for n in range(1, NC):
         planar_part(order[n])
-    for row in range(part):
-        coef_out[row] = jnp.dot(
-            wv[...], zfull[row], precision=HIGHEST, preferred_element_type=jnp.float32
-        )
-
     for copy in stores:
         copy.wait()
     for kind in range(4):
@@ -447,6 +441,24 @@
         for f in range(len(FLOWS)):
             for o in range(slabs):
                 sent(sum_copy(f, o, None, c))
+
+
+def finish_kernel(pieces, field, planar, wz, next_out, coef_out, coef, sem):
+    n = field.shape[0] // pieces
+    copies = [
+        pltpu.make_async_copy(field.at[pl.ds(i * n, n)], next_out.at[pl.ds(i * n, n)], sem.at[i])
+        for i in range(pieces)
+    ]
+    for c in copies:
+        c.start()
+    for row in range(planar.shape[0]):
+        coef[row] = jnp.dot(
+            wz[...], planar[row], precision=HIGHEST, preferred_element_type=jnp.float32
+        )
+        copies.append(pltpu.make_async_copy(coef.at[row], coef_out.at[row], sem.at[pieces + row]))
+        copies[-1].start()
+    for c in copies:
+        c.wait()
 
 
 def pin(array):
@@ -466,13 +478,13 @@
     f32 = jnp.float32
     vmem = lambda *shape: pltpu.VMEM(shape, f32)
     dma = lambda *shape: pltpu.SemaphoreType.DMA(shape)
-    return pl.pallas_call(
+    field, planar = pl.pallas_call(
         functools.partial(kernel, strips, slabs, used),
         out_shape=(
             jax.ShapeDtypeStruct((X, Z, Y), f32),
             jax.ShapeDtypeStruct((HX // slabs, depth, Y // 2), f32),
         ),
-        in_specs=[hbm] * 9,
+        in_specs=[hbm] * 8,
         out_specs=(hbm, pl.BlockSpec(memory_space=pltpu.VMEM)),
         scratch_shapes=[
             vmem(X + 7, Z + 2 * HALO, Y),
@@ -485,12 +497,10 @@
             vmem(Y, Y),
             vmem(Y, Y),
             vmem(Y, Y),
-            vmem(depth, depth),
             vmem(NC, len(SLOTS), HC, Y // 2),
             vmem(NC, slabs, places, HC, Y // 2),
-            vmem(HX // slabs, depth, Y // 2),
             pltpu.SMEM(table.shape, f32),
-            dma(9 + 2 * NC),
+            dma(8 + 2 * NC),
             dma(5, NC),
             dma(5, NC),
             dma(4),
@@ -503,8 +513,21 @@
         ),
     )(
         pin(current), pin(previous), pin(stiffness), pin(buoyancy),
-        pin(table), pin(grad), pin(div), pin(lift), pin(z_matrix(depth)),
+        pin(table), pin(grad), pin(div), pin(lift),
     )
+    vspec = pl.BlockSpec(memory_space=pltpu.VMEM)
+    pieces = 4
+    return pl.pallas_call(
+        functools.partial(finish_kernel, pieces),
+        out_shape=(
+            jax.ShapeDtypeStruct((X, Z, Y), f32),
+            jax.ShapeDtypeStruct((part, depth, Y // 2), f32),
+        ),
+        in_specs=[pl.BlockSpec(memory_space=pl.ANY), vspec, vspec],
+        out_specs=(pl.BlockSpec(memory_space=pl.ANY),) * 2,
+        scratch_shapes=[vmem(part, depth, Y // 2), dma(pieces + part)],
+        compiler_params=pltpu.CompilerParams(vmem_limit_bytes=16 * 1024 * 1024),
+    )(field, planar, z_matrix(depth))
 
 
 def solution(mesh):

time: 26.5 us -> 24.6 us (0.928)
  the two profiles are of different devices: /device:TPU:1 before, /device:TPU:11 now
where the time goes in v4:
time: 24.6 us; the launch traced here: 24.3 us
  Pallas kernels  23.7 us (96%)
  between operations  0.65 us (3%)
    pallas_call x1, Pallas kernels, on_device(): pl.pallas_call(functools.partial(kernel, strips, slabs, used), out_shape=...  22.6 us
    pallas_call x1, Pallas kernels, on_device(): pl.pallas_call(functools.partial(finish_kernel, pieces), out_shape=(jax.S...  1.07 us

profile of v4, /device:TPU:11, one launch (start us, length us, event | category | flops | bytes accessed | tf_op | source)
XLA Modules:
  0.0 24.3 jit_solution(10560046111569231344)
XLA Ops:
  0.6 0.0 copy-start
  0.6 22.6 %shard_map.104 = (f32[16,64,256]{2,1,0:T(8,128)S(1)}, f32[4,64,128]{2,1,0:T(8,128)S(1)}) custom-call(f32[16,64,256]{2,1,0:T(8,128)} %cur.1, f32[16,64,256]{2,1,0:T(8,128)} %prev.1, f32[16,64,256]{2,1,0:T(8,128)} %stiff.1, f32[16,64,256]{2,1,0:T(8,128)} %buoy.1, f32[5,352]{1,0:T(8,128)} %constant.10.clone.weights, f32[256,256]{1,0:T(8,128)} %constant.11.clone.gy, ...), custom_call_target="tpu_custom_call" | custom-call | tf_op jit(solution)/shard_map/pallas_call | solution.py:481
  23.2 0.0 copy-done
  23.3 1.1 %shard_map.105 = (f32[16,64,256]{2,1,0:T(8,128)}, f32[4,64,128]{2,1,0:T(8,128)}) custom-call(f32[16,64,256]{2,1,0:T(8,128)S(1)} %get-tuple-element.4.field, f32[4,64,128]{2,1,0:T(8,128)S(1)} %get-tuple-element.5.planar, f32[64,64]{1,0:T(8,128)S(1)} %copy-done), custom_call_target="tpu_custom_call" | custom-call | tf_op jit(solution)/shard_map/pallas_call | solution.py:520
Async XLA Ops:
  0.6 22.6 %copy-start = (f32[64,64]{1,0:T(8,128)S(1)}, f32[64,64]{1,0:T(8,128)}, u32[]{:S(2)}) copy-start(f32[64,64]{1,0:T(8,128)} %constant.14.clone.wz) | copy-start | bytes 49156
